TPU v7x, 256 devices: a whole 4x4x8 slice. The times are simulated.
256 devices in a mesh: seq: 32 (over y, z), grp: 8 (over x, core).
Axes of the slice: x: 4, y: 4, z: 8, core: 2. Of those that a mesh axis runs over, the one named last changes fastest.
Arguments:
- activations: bfloat16 [32768, 4096], P(('grp', 'seq')), parts along dimension 0, may hold values from -6 to 6
- input_weight: bfloat16 [16, 256, 256], replicated, may hold values from -0.375 to 0.375
- decay_weight: bfloat16 [16, 256, 256], replicated, may hold values from -0.375 to 0.375
- input_bias: float32 [4096], replicated, may hold values from -4 to 4
- decay_bias: float32 [4096], replicated, may hold values from -4 to 4
- decay_logits: float32 [4096], replicated, may hold values from -16 to -3
- doc_lengths: int32 [48], P('grp'), parts along dimension 0, may hold values from 1 to 2048, 4096 in all
- cotangent: bfloat16 [32768, 4096], P(('grp', 'seq')), parts along dimension 0, may hold values from -6 to 6
Outputs:
- states: bfloat16 [32768, 4096], P(('grp', 'seq')), parts along dimension 0
- input_grads: bfloat16 [32768, 4096], P(('grp', 'seq')), parts along dimension 0
- input_weight_grads: float32 [32768, 256], P(('grp', 'seq')), parts along dimension 0
- decay_weight_grads: float32 [32768, 256], P(('grp', 'seq')), parts along dimension 0
- input_bias_grads: float32 [32768], P(('grp', 'seq')), parts along dimension 0
- decay_bias_grads: float32 [32768], P(('grp', 'seq')), parts along dimension 0
- decay_logits_grads: float32 [32768], P(('grp', 'seq')), parts along dimension 0
There are 8 independent parts, one for each index of `grp`. A program takes and returns all parts, laid end to end along the dimension named above; an argument that names none is the same for every part. Nothing has to cross between parts.
Inputs may be any that keep to these rules, and one draw needn't show every extreme that they name: `doc_lengths`: the lengths sum to 4096.
All inputs are finite; a program needn't handle non-finite values.
Results may differ from a plain program's by a relative error of at most 0.0034.
Values may be sent and summed in bfloat16 or wider, within the bound.
A program may use at most 128 MiB of HBM per device.

v0:
```python
import math

import jax
import jax.numpy as jnp
from jax import lax
from jax.sharding import PartitionSpec as P

DECAY_SCALE = 8.0
SQRT_FLOOR = 2.5e-07


def carried_in(x, axis, combine, identity, reverse):
    devices, place = (lax.axis_size(axis), lax.axis_index(axis))
    everything = jax.tree.map(lambda part: lax.all_gather(part, axis), x)
    start = jax.tree.map(
        lambda part, zero: jnp.broadcast_to(jnp.asarray(zero, part.dtype), part.shape), x, identity
    )

    def hop(k, before):
        at = devices - 1 - k if reverse else k
        reached = at > place if reverse else at < place
        new = combine(before, jax.tree.map(lambda part: part[at], everything))
        return jax.tree.map(lambda a, b: jnp.where(reached, a, b), new, before)

    return lax.fori_loop(0, devices, hop, start)


def affine_pair(earlier, later):
    return (earlier[0] * later[0], later[0] * earlier[1] + later[1])


def per_block(left, weight):
    rows = left.shape[0]
    heads = weight.shape[0]
    width = weight.shape[1]
    shaped = left.reshape(rows, heads, width)
    return jnp.einsum("thi,hij->thj", shaped, weight, preferred_element_type=jnp.float32).reshape(
        rows, heads * width
    )


def per_block_back(grads, weight):
    rows = grads.shape[0]
    heads = weight.shape[0]
    width = weight.shape[1]
    shaped = grads.reshape(rows, heads, width)
    return jnp.einsum("thj,hij->thi", shaped, weight, preferred_element_type=jnp.float32).reshape(
        rows, heads * width
    )


def local_chain(factors, values, reverse):
    rows = factors.shape[0]
    width = factors.shape[1]
    group = math.gcd(rows, 16)
    fac3 = factors.reshape(rows // group, group, width)
    val3 = values.reshape(rows // group, group, width)
    order = list(range(group))
    if reverse:
        order = order[::-1]

    def advance(carry, blocks):
        running_prod, running_sum = carry
        fac_block, val_block = blocks
        prods = [None] * group
        sums = [None] * group
        for place in order:
            running_prod = fac_block[place] * running_prod
            running_sum = fac_block[place] * running_sum + val_block[place]
            prods[place] = running_prod
            sums[place] = running_sum
        return ((running_prod, running_sum), (jnp.stack(prods, axis=0), jnp.stack(sums, axis=0)))

    start = (jnp.ones((width,), jnp.float32), jnp.zeros((width,), jnp.float32))
    _, (all_prods, all_sums) = lax.scan(advance, start, (fac3, val3), reverse=reverse)
    return (all_prods.reshape(rows, width), all_sums.reshape(rows, width))


def on_device(
    activations,
    input_weight,
    decay_weight,
    input_bias,
    decay_bias,
    decay_logits,
    doc_lengths,
    cotangent,
):
    rows = activations.shape[0]
    width_all = activations.shape[1]
    heads = input_weight.shape[0]
    block = input_weight.shape[1]
    here = lax.axis_index("seq")
    starts = jnp.cumsum(doc_lengths) - doc_lengths
    position = here * rows + jnp.arange(rows, dtype=jnp.int32)
    reset = jnp.any(position[:, None] == starts[None, :], axis=1).astype(jnp.float32)[:, None]
    keep = 1.0 - reset
    input_gate = jax.nn.sigmoid(per_block(activations, input_weight) + input_bias)
    decay_gate = jax.nn.sigmoid(per_block(activations, decay_weight) + decay_bias)
    softened = jax.nn.softplus(decay_logits)
    log_decay = -DECAY_SCALE * decay_gate * softened
    decay = jnp.exp(log_decay)
    complement = -jnp.expm1(2.0 * log_decay)
    multiplier = jnp.where(reset > 0.0, 1.0, jnp.sqrt(complement))
    factor = keep * decay
    inputs = activations.astype(jnp.float32)
    pushed = inputs * input_gate * multiplier
    prefix, local_state = local_chain(factor, pushed, False)
    following = jnp.concatenate([factor[1:], jnp.ones_like(factor[:1])], axis=0)
    upstream = cotangent.astype(jnp.float32)
    tail_prod, tail_sum = local_chain(following, upstream, True)
    head_prod = factor[0] * tail_prod[0]
    head_sum = factor[0] * tail_sum[0]
    ones_row = jnp.ones((width_all,), jnp.float32)
    zeros_row = jnp.zeros((width_all,), jnp.float32)
    carry_in = carried_in(
        (prefix[-1], local_state[-1]), "seq", affine_pair, (ones_row, zeros_row), False
    )[1]
    back_in = carried_in((head_prod, head_sum), "seq", affine_pair, (ones_row, zeros_row), True)[1]
    hidden = local_state + prefix * carry_in
    states = hidden.astype(jnp.bfloat16)
    previous = jnp.concatenate([carry_in[None], hidden[:-1]], axis=0)
    carried = tail_sum + tail_prod * back_in
    dmult = carried * inputs * input_gate
    d_log = keep * (
        carried * previous * decay
        - decay * decay * dmult / jnp.sqrt(jnp.maximum(complement, SQRT_FLOOR))
    )
    pre_input = carried * inputs * multiplier * input_gate * (1.0 - input_gate)
    pre_decay = -DECAY_SCALE * softened * d_log * decay_gate * (1.0 - decay_gate)
    low_input = pre_input.astype(jnp.bfloat16)
    low_decay = pre_decay.astype(jnp.bfloat16)
    input_grads = (
        carried * input_gate * multiplier
        + per_block_back(low_input, input_weight)
        + per_block_back(low_decay, decay_weight)
    )
    input_grads = input_grads.astype(jnp.bfloat16)
    bias_input = jnp.sum(pre_input, axis=0)
    bias_decay = jnp.sum(pre_decay, axis=0)
    logit_term = jnp.sum(-DECAY_SCALE * decay_gate * d_log, axis=0) * jax.nn.sigmoid(decay_logits)
    act3 = activations.reshape(rows, heads, block)
    term_input = jnp.einsum(
        "thi,thj->hij",
        act3,
        low_input.reshape(rows, heads, block),
        preferred_element_type=jnp.float32,
    ).reshape(width_all, block)
    term_decay = jnp.einsum(
        "thi,thj->hij",
        act3,
        low_decay.reshape(rows, heads, block),
        preferred_element_type=jnp.float32,
    ).reshape(width_all, block)
    grad_in_w, grad_dec_w, grad_in_b, grad_dec_b, grad_logit = (
        lax.psum_scatter(term_input, "seq", scatter_dimension=0, tiled=True),
        lax.psum_scatter(term_decay, "seq", scatter_dimension=0, tiled=True),
        lax.psum_scatter(bias_input, "seq", scatter_dimension=0, tiled=True),
        lax.psum_scatter(bias_decay, "seq", scatter_dimension=0, tiled=True),
        lax.psum_scatter(logit_term, "seq", scatter_dimension=0, tiled=True),
    )
    return (states, input_grads, grad_in_w, grad_dec_w, grad_in_b, grad_dec_b, grad_logit)


def solution(mesh):
    in_specs = (P(("grp", "seq"), None), P(), P(), P(), P(), P(), P("grp"), P(("grp", "seq"), None))
    out_specs = (
        P(("grp", "seq"), None),
        P(("grp", "seq"), None),
        P(("grp", "seq"), None),
        P(("grp", "seq"), None),
        P(("grp", "seq")),
        P(("grp", "seq")),
        P(("grp", "seq")),
    )
    return jax.shard_map(
        on_device, mesh=mesh, in_specs=in_specs, out_specs=out_specs, check_vma=False
    )
```

profile of v0, /device:TPU:2, one launch (start us, length us, event | category | flops | bytes accessed | tf_op | source)
XLA Modules:
  0.0 1003.3 jit_solution(12556269996201319120)
XLA Ops:
  21.8 3.8 fusion.29
  28.6 4.0 exponential_multiply_fusion
  32.6 5.7 exponential_multiply_fusion.1
  41.4 115.8 %while.68 = (s32[]{:T(128)}, f32[4096]{0:T(1024)}, f32[4096]{0:T(1024)}, f32[8,16,4096]{2,1,0:T(8,128)}, f32[8,16,4096]{2,1,0:T(8,128)}, /*index=5*/f32[8,16,409...) while((s32[]{:T(128)}, f32[4096]{0:T(1024)}, ...), condition=%wide.region_3.4_spmd.clone, body=%wide.region_2.3_spmd.clone.sunk | while | flops 204818 | bytes 4489760 | solution.py:75
  49.8 3.2 stack.481
  64.5 3.2 stack.481
  79.2 3.2 stack.481
  152.2 3.2 stack.481
  158.1 52.8 %all-gather = f32[32,1,4096]{2,1,0:T(1,128)S(1)} all-gather(f32[1,1,4096]{2,1,0:T(1,128)S(1)} %slice_bitcast_fusion.1), channel_id=1, replica_groups=mesh['seq'=32,'grp'=8] {'seq'}, dimensions={0}, use_global_device_ids=true | all-gather | bytes 540672 | tf_op jit(solution)/shard_map/all_gather | solution.py:14
  212.9 48.5 %all-gather.1 = f32[32,1,4096]{2,1,0:T(1,128)S(1)} all-gather(f32[1,1,4096]{2,1,0:T(1,128)S(1)} %slice_bitcast_fusion), channel_id=1, replica_groups=mesh['seq'=32,'grp'=8] {'seq'}, dimensions={0}, use_global_device_ids=true | all-gather | bytes 540672 | tf_op jit(solution)/shard_map/all_gather | solution.py:14
  262.6 33.3 %while.69 = (s32[]{:T(128)}, f32[4096]{0:T(1024)S(1)}, s32[]{:T(128)}, f32[32,4096]{1,0:T(8,128)}, f32[32,4096]{1,0:T(8,128)}, /*index=5*/s32[]{:T(128)}, s32[]{:T(128)}) while((s32[]{:T(128)}, f32[4096]{0:T(1024)S(1)}, s32[]{:T(128)}, f32[32,4096]{1,0:T(8,128)}, f32[32,4096]{1,0:T(8,128)}, /*index=5*/s32[]{:T(128)}, ...), condition=%wide.region_5.6_spmd.clone, body=%wide.region_4.5_spmd.clone.sunk | while | flops 16388 | bytes 131181 | solution.py:25
  295.9 4.4 fusion.27
  307.7 100.3 %while.70 = (s32[]{:T(128)}, f32[4096]{0:T(1024)S(1)}, f32[4096]{0:T(1024)S(1)}, f32[8,16,4096]{2,1,0:T(8,128)}, f32[8,16,4096]{2,1,0:T(8,128)}, /*index=5*/f32[...) while((s32[]{:T(128)}, f32[4096]{0:T(1024)S(1)}, ...), condition=%wide.region_7.8_spmd.clone, body=%wide.region_6.7_spmd.clone.sunk | while | flops 204819 | bytes 4489780 | solution.py:75
  409.2 47.2 %all-gather.2 = f32[32,1,4096]{2,1,0:T(1,128)S(1)} all-gather(f32[1,1,4096]{2,1,0:T(1,128)S(1)} %get-tuple-element.723), channel_id=1, replica_groups=mesh['seq'=32,'grp'=8] {'seq'}, dimensions={0}, use_global_device_ids=true | all-gather | bytes 540672 | tf_op jit(solution)/shard_map/all_gather | solution.py:14
  457.5 48.3 %all-gather.3 = f32[32,1,4096]{2,1,0:T(1,128)S(1)} all-gather(f32[1,1,4096]{2,1,0:T(1,128)S(1)} %get-tuple-element.722), channel_id=1, replica_groups=mesh['seq'=32,'grp'=8] {'seq'}, dimensions={0}, use_global_device_ids=true | all-gather | bytes 540672 | tf_op jit(solution)/shard_map/all_gather | solution.py:14
  506.9 33.5 %while.71 = (s32[]{:T(128)}, f32[4096]{0:T(1024)S(1)}, s32[]{:T(128)}, f32[32,4096]{1,0:T(8,128)}, f32[32,4096]{1,0:T(8,128)}, /*index=5*/s32[]{:T(128)}, s32[]{:T(128)}, s32[]{:T(128)}, s32[]{:T(128)}) while((s32[]{:T(128)}, f32[4096]{0:T(1024)S(1)}, s32[]{:T(128)}, f32[32,4096]{1,0:T(8,128)}, f32[32,4096]{1,0:T(8,128)}, ...), condition=%wide.region_9.10_spmd.clone, body=%wide.region_8.9_spmd.clone.sunk | while | flops 16392 | bytes 131243 | solution.py:25
  540.4 6.2 multiply_reduce_fusion
  546.7 3.7 fusion.26
  553.4 3.9 fusion.6
  566.6 3.8 convolution_bitcast_fusion.1
  577.5 140.6 %all-reduce.4 = (f32[4096]{0:T(1024)S(1)}, f32[4096]{0:T(1024)S(1)}, f32[4096]{0:T(1024)S(1)}) all-reduce(f32[4096]{0:T(1024)S(1)} %get-tuple-element.643, f32[4096]{0:T(1024)S(1)} %get-tuple-element.525, f32[4096]{0:T(1024)S(1)} %divide_multiply_fusion), channel_id=4, replica_groups=mesh['seq'=32,'grp'=8] {'seq'}, use_global_device_ids=true, to_apply=%region_13.14.clone | all-reduce | flops 12288 | bytes 98304
  719.8 7.4 add_convert_fusion
  727.2 44.9 %reduce-scatter.3.cloned.1.call-done = f32[128,256]{1,0:T(8,128)} async-done(((f32[4096,256]{1,0:T(8,128)}), f32[128,256]{1,0:T(8,128)}) %reduce-scatter.3.cloned.1.call-update) | async-done | bytes 131088 | tf_op jit(solution)/shard_map/reduce_scatter | solution.py:156
  772.1 224.4 %reduce-scatter.5.cloned.1.call-done = f32[128,256]{1,0:T(8,128)} async-done(((f32[4096,256]{1,0:T(8,128)}), f32[128,256]{1,0:T(8,128)}) %reduce-scatter.5.cloned.1.call-update) | async-done | bytes 131088 | tf_op jit(solution)/shard_map/reduce_scatter | solution.py:157
  (343 shorter events, 323.1 us)
Async XLA Ops:
  7.2 3.5 copy-start
  7.2 764.9 %reduce-scatter.3.cloned.1.call-start = ((), (), s32[]{:S(2)}) async-start(), calls=%async_computation.2 | async-start | bytes 4325376 | tf_op jit(solution)/shard_map/reduce_scatter | solution.py:156
  9.0 23.5 %copy-start.26 = (f32[128]{0:T(128)}, f32[128]{0:T(128)S(1)}, u32[]{:S(2)}) copy-start(f32[128]{0:T(128)S(1)} %convert_subtract_fusion) | copy-start | bytes 1540
  9.0 23.5 %copy-start.24 = (pred[128]{0:T(512)(128)(4,1)}, pred[128]{0:T(512)(128)(4,1)S(1)}, u32[]{:S(2)}) copy-start(pred[128]{0:T(512)(128)(4,1)S(1)} %convert_compare_fusion) | copy-start | bytes 388
  18.8 13.7 %copy-start.15 = (f32[4096]{0:T(1024)}, f32[4096]{0:T(1024)S(1)}, u32[]{:S(2)}) copy-start(f32[4096]{0:T(1024)S(1)} %fusion.18) | copy-start | bytes 49156
  28.5 4.0 copy-start.1
  28.5 4.0 copy-start.3
  28.5 4.0 copy-start.20
  157.2 105.4 %copy-start.12 = (f32[4096]{0:T(1024)S(1)}, f32[4096]{0:T(1024)}, u32[]{:S(2)}) copy-start(f32[4096]{0:T(1024)} %custom-call.2) | copy-start | bytes 49156
  295.9 4.4 copy-start.13
  295.9 4.4 copy-start.10
  408.0 98.8 %copy-start.17 = (f32[4096]{0:T(1024)S(1)}, f32[4096]{0:T(1024)}, u32[]{:S(2)}) copy-start(f32[4096]{0:T(1024)} %custom-call.5) | copy-start | bytes 49156
  408.0 132.3 %copy-start.14 = (f32[4096]{0:T(1024)S(1)}, f32[4096]{0:T(1024)}, u32[]{:S(2)}) copy-start(f32[4096]{0:T(1024)} %copy-done.13) | copy-start | bytes 49156
  408.0 132.3 %copy-start.16 = (f32[4096]{0:T(1024)S(1)}, f32[4096]{0:T(1024)}, u32[]{:S(2)}) copy-start(f32[4096]{0:T(1024)} %copy-done.15) | copy-start | bytes 49156
  408.0 132.3 %copy-start.19 = (f32[4096]{0:T(1024)S(1)}, f32[4096]{0:T(1024)}, u32[]{:S(2)}) copy-start(f32[4096]{0:T(1024)} %param.20) | copy-start | bytes 49156
  408.0 132.3 %copy-start.21 = (f32[4096]{0:T(1024)S(1)}, f32[4096]{0:T(1024)}, u32[]{:S(2)}) copy-start(f32[4096]{0:T(1024)} %param.19) | copy-start | bytes 49156
  408.1 132.3 %copy-start.27 = (f32[128]{0:T(128)S(1)}, f32[128]{0:T(128)}, u32[]{:S(2)}) copy-start(f32[128]{0:T(128)} %copy-done.26) | copy-start | bytes 1540
  540.4 6.3 copy-start.2
  540.4 6.3 copy-start.4
  540.4 6.3 copy-start.6
  540.4 6.3 copy-start.25
  546.7 3.8 copy-start.5
  553.1 443.4 %reduce-scatter.5.cloned.1.call-start = ((), (), s32[]{:S(2)}) async-start(), calls=%async_computation.3 | async-start | bytes 4325376 | tf_op jit(solution)/shard_map/reduce_scatter | solution.py:157
  573.3 4.2 copy-start.23
  (7 other events, 16.8 us)
Sparse Core Ops, SparseCore 0:
  553.2 218.8 reduce-scatter.2
  777.1 219.3 reduce-scatter.4
where the time goes:
time: 1010 us; the launch traced here: 1000 us
  blocking collectives  337 us (33%)
  local copies, waits for them, and re-layouts  290 us (29%)
  waiting for transfers between devices  269 us (27%)
  other arithmetic  70.3 us (7%)
  matrix products  18.4 us (2%)
  between operations  15.1 us (1%)
    reduce_scatter x1, waiting for transfers between devices, on_device(): lax.psum_scatter(term_decay, 'seq', scatter_dimension=0, tiled=True)  224 us
    all_gather x4, blocking collectives, carried_in(): everything = jax.tree.map(lambda part: lax.all_gather(part, axis), x)  197 us
    unnamed x1, blocking collectives  141 us
    dynamic_slice x64, local copies, waits for them, and re-layouts, hop(): new = combine(before, jax.tree.map(lambda part: part[at], everything))  63.8 us
    another operation x16, local copies, waits for them, and re-layouts, advance(): jnp.stack(prods, axis=0)  45.9 us
    reduce_scatter x1, waiting for transfers between devices, on_device(): lax.psum_scatter(term_input, 'seq', scatter_dimension=0, tiled=True)  44.9 us
    slice x16, local copies, waits for them, and re-layouts, advance(): running_prod = fac_block[place] * running_prod  37.4 us
    slice x16, local copies, waits for them, and re-layouts, advance(): running_sum = fac_block[place] * running_sum + val_block[place]  37.3 us
  transfers between devices with their start and end apart: 2, of which 2 were waited for; matrix products, arithmetic and copies ran while one was open for 3% of the time, Pallas kernels for 0%

commit v1 on v0

v1 whole, which is shorter than its diff:
```python
import jax
import jax.numpy as jnp
from jax import lax
from jax.experimental import pallas as pl
from jax.experimental.pallas import tpu as pltpu
from jax.sharding import PartitionSpec as P

ROWS = 128
WIDTH = 4096
HEADS = 16
BW = 256
DOCS = 6
RING_Y = 4
RING_Z = 8
SEQ_DEVICES = RING_Y * RING_Z
STEPS = 16
GROUPS = 4
ROWS_ZY = 48
ROWS_YZ = ROWS - ROWS_ZY
DECAY_SCALE = 8.0
ROOT_LIMIT = 2000.0
TINY = 1.2e-38
MESH = pl.DeviceIdType.MESH
F32 = jnp.float32
BF16 = jnp.bfloat16

Z_CHAINS = ((0, 1, 4), (0, -1, 3), (1, 1, 3), (1, -1, 4))
Y_CHAINS = ((0, 1, 2), (0, -1, 1), (1, 1, 1), (1, -1, 2))
Z_SUBS = ((4, 3), (-3, 2), (-2, 1), (-1, 0))


def slots_of(chains):
    table, count = {}, 0
    for c, (_, _, hops) in enumerate(chains):
        for i in range(hops):
            table[(c, i)] = count
            count += 1
    return table, count


Z_SLOT, Z_COUNT = slots_of(Z_CHAINS)
Y_SLOT, Y_COUNT = slots_of(Y_CHAINS)


def dot(a, b, dims=((1,), (0,))):
    return lax.dot_general(a, b, (dims, ((), ())), preferred_element_type=F32)


def tile_of(rows):
    pad = jnp.zeros((8 - len(rows), rows[0].shape[1]), F32)
    return jnp.concatenate(list(rows) + [pad], axis=0)


def kernel(
    docs_ref,
    act_hbm,
    wi_hbm,
    wd_hbm,
    bi_ref,
    bd_ref,
    logit_ref,
    cot_hbm,
    states_hbm,
    grads_hbm,
    wgi_ref,
    wgd_ref,
    vec_ref,
    act_v,
    cot_v,
    wi_v,
    wd_v,
    actp,
    cotp,
    fac,
    psh,
    coef,
    quo,
    gin,
    dgate,
    u_s,
    keep_s,
    k8_s,
    perm_s,
    permt_s,
    seg_s,
    states_v,
    grads_v,
    part,
    map_send,
    map_recv,
    rep_send,
    rep_recv,
    bias_send,
    bias_recv,
    z1s,
    z1r,
    y1s,
    y1r,
    z2s,
    z2r,
    y2s,
    y2r,
    in_sem,
    out_sem,
    small_sem,
    z1_ss,
    z1_rs,
    y1_ss,
    y1_rs,
    z2_ss,
    z2_rs,
    y2_ss,
    y2_rs,
):
    me = lax.axis_index("seq")
    y, z = me // RING_Z, lax.rem(me, RING_Z)

    gw = WIDTH // GROUPS
    gh = HEADS // GROUPS
    fetches = []
    for g in range(GROUPS):
        cols = pl.ds(g * gw, gw)
        heads = pl.ds(g * gh, gh)
        pairs = (
            (act_hbm.at[:, cols], act_v.at[:, cols]),
            (wi_hbm.at[heads], wi_v.at[heads]),
            (wd_hbm.at[heads], wd_v.at[heads]),
            (cot_hbm.at[:, cols], cot_v.at[:, cols]),
        )
        group = [
            pltpu.make_async_copy(s, d, in_sem.at[g, i]) for i, (s, d) in enumerate(pairs)
        ]
        for c in group:
            c.start()
        fetches.append(group)

    barrier = pltpu.get_barrier_semaphore()

    def hello(i, carry):
        pl.semaphore_signal(
            barrier,
            inc=1,
            device_id={"seq": lax.rem(me + i, SEQ_DEVICES)},
            device_id_type=MESH,
        )
        return carry

    lax.fori_loop(1, SEQ_DEVICES, hello, 0)

    row = lax.broadcasted_iota(jnp.int32, (ROWS, ROWS), 0)
    col = lax.broadcasted_iota(jnp.int32, (ROWS, ROWS), 1)
    perm_s[...] = (col == (row & 7) * STEPS + (row >> 3)).astype(F32).astype(BF16)
    permt_s[...] = (row == (col & 7) * STEPS + (col >> 3)).astype(F32).astype(BF16)
    seg = lax.broadcasted_iota(jnp.int32, (8, BW), 0)
    first = me * ROWS + seg * STEPS
    starts = [jnp.int32(0)]
    for j in range(DOCS - 1):
        starts.append(starts[-1] + docs_ref[j])
    for k in range(STEPS):
        hit = first + k == starts[0]
        for j in range(1, DOCS):
            hit = hit | (first + k == starts[j])
        keep_s[8 * k : 8 * k + 8, :] = jnp.where(hit, 0.0, 1.0)
    logits = logit_ref[...]
    e = jnp.exp(-jnp.abs(logits))
    series = e * (1.0 + e * (-1 / 2 + e * (1 / 3 + e * (-1 / 4 + e * (1 / 5 + e * (-1 / 6))))))
    soft = jnp.maximum(logits, 0.0) + jnp.where(e < 0.0625, series, jnp.log(1.0 + e))
    k8_s[...] = -DECAY_SCALE * soft

    pl.semaphore_wait(barrier, SEQ_DEVICES - 1)

    def send_tile(src, dst, send_sem, recv_sem, to):
        @pl.when(to != me)
        def _():
            pltpu.make_async_remote_copy(
                src_ref=src.at[to],
                dst_ref=dst.at[me],
                send_sem=send_sem,
                recv_sem=recv_sem,
                device_id={"seq": to},
                device_id_type=MESH,
            ).start()

    def wait_tiles(buf, sem):
        view = buf.at[pl.ds(0, SEQ_DEVICES - 1)]
        pltpu.make_async_copy(view, view, sem).wait()

    def lanes(h):
        return pl.ds(pl.multiple_of(h * BW, BW), BW)

    def phase_a(h, carry):
        sl = lanes(h)
        x = dot(perm_s[...], act_v[:, sl])
        xb = x.astype(BF16)
        actp[h] = xb
        ct = dot(perm_s[...], cot_v[:, sl])
        cotp[h] = ct
        gi = dot(xb, wi_v[h]) + bi_ref[:, sl]
        gd = dot(xb, wd_v[h]) + bd_ref[:, sl]
        k8 = k8_s[:, sl]
        prod = jnp.ones((8, BW), F32)
        fwd = jnp.zeros((8, BW), F32)
        bwd = jnp.zeros((8, BW), F32)
        for k in range(STEPS):
            r = slice(8 * k, 8 * k + 8)
            alive = keep_s[r, :] > 0.0
            xk = x[r]
            ig = 1.0 / (1.0 + jnp.exp(-gi[r]))
            dg = 1.0 / (1.0 + jnp.exp(-gd[r]))
            ld = dg * k8
            dec = jnp.exp(ld)
            t = ld + ld
            near = -t * (1.0 + t * (1 / 2 + t * (1 / 6 + t * (1 / 24))))
            comp = jnp.where(t > -0.0625, near, 1.0 - dec * dec)
            root = lax.rsqrt(jnp.maximum(comp, TINY))
            mult = jnp.where(alive, comp * root, 1.0)
            f = jnp.where(alive, dec, 0.0)
            a = ig * mult
            p = xk * a
            fac[h, r, :] = f
            psh[h, r, :] = p
            coef[h, r, :] = a
            quo[h, r, :] = dec * xk * ig * jnp.minimum(root, ROOT_LIMIT)
            gin[h, r, :] = p * (1.0 - ig)
            dgate[h, r, :] = dg
            fwd = f * fwd + p
            prod = prod * f
            bwd = bwd + prod * ct[r]
        fa, ba = prod, prod
        for d in (1, 2, 4):
            later = seg >= d
            fwd = jnp.where(later, fa * pltpu.roll(fwd, d, 0) + fwd, fwd)
            fa = jnp.where(later, fa * pltpu.roll(fa, d, 0), fa)
            earlier = seg < 8 - d
            bwd = jnp.where(earlier, ba * pltpu.roll(bwd, 8 - d, 0) + bwd, bwd)
            ba = jnp.where(earlier, ba * pltpu.roll(ba, 8 - d, 0), ba)
        whole = tile_of((fa[7:8], fwd[7:8], bwd[0:1]))
        seg_s[h, 0] = jnp.where(seg == 0, 1.0, pltpu.roll(fa, 1, 0))
        seg_s[h, 1] = jnp.where(seg == 0, 0.0, pltpu.roll(fwd, 1, 0))
        seg_s[h, 2] = jnp.where(seg == 7, 1.0, pltpu.roll(ba, 7, 0))
        seg_s[h, 3] = jnp.where(seg == 7, 0.0, pltpu.roll(bwd, 7, 0))
        for half in range(2):
            to = 2 * h + half
            piece = whole[:, half * ROWS : (half + 1) * ROWS]
            map_send[to] = piece

            @pl.when(to == me)
            def _():
                map_recv[me] = piece

            send_tile(map_send, map_recv, small_sem.at[0], small_sem.at[1], to)
        return carry

    for g in range(GROUPS):
        for c in fetches[g]:
            c.wait()
        lax.fori_loop(g * gh, (g + 1) * gh, phase_a, 0)

    wait_tiles(map_recv, small_sem.at[1])
    hid = jnp.zeros((1, ROWS), F32)
    for s in range(SEQ_DEVICES):
        rep_send[s, 0:1, :] = hid
        hid = map_recv[s, 0:1, :] * hid + map_recv[s, 1:2, :]
    back = jnp.zeros((1, ROWS), F32)
    for s in reversed(range(SEQ_DEVICES)):
        rep_send[s, 1:2, :] = back
        back = map_recv[s, 0:1, :] * back + map_recv[s, 2:3, :]
    rep_recv[me] = rep_send[me]

    def reply(i, carry):
        send_tile(
            rep_send, rep_recv, small_sem.at[2], small_sem.at[3], lax.rem(me + i, SEQ_DEVICES)
        )
        return carry

    lax.fori_loop(1, SEQ_DEVICES, reply, 0)
    wait_tiles(rep_recv, small_sem.at[3])

    def phase_b(h, carry):
        sl = lanes(h)
        t0, t1 = rep_recv[2 * h], rep_recv[2 * h + 1]
        hin = jnp.concatenate([t0[0:1], t1[0:1]], axis=1)
        cin = jnp.concatenate([t0[1:2], t1[1:2]], axis=1)
        hid = seg_s[h, 0] * hin + seg_s[h, 1]
        c = seg_s[h, 2] * cin + seg_s[h, 3]
        for k in reversed(range(STEPS)):
            r = slice(8 * k, 8 * k + 8)
            u = cotp[h, r, :] + c
            u_s[r, :] = u
            c = fac[h, r, :] * u
        k8 = k8_s[:, sl]
        sum_i = jnp.zeros((8, BW), F32)
        sum_d = jnp.zeros((8, BW), F32)
        sum_l = jnp.zeros((8, BW), F32)
        hids, lows_i, lows_d, direct = [], [], [], []
        for k in range(STEPS):
            r = slice(8 * k, 8 * k + 8)
            u = u_s[r, :]
            f = fac[h, r, :]
            dg = dgate[h, r, :]
            dl = f * u * (hid - quo[h, r, :]) * dg
            pd = k8 * dl * (1.0 - dg)
            pi = u * gin[h, r, :]
            hid = f * hid + psh[h, r, :]
            sum_i = sum_i + pi
            sum_d = sum_d + pd
            sum_l = sum_l + dl
            hids.append(hid)
            lows_i.append(pi)
            lows_d.append(pd)
            direct.append(u * coef[h, r, :])
        low_i = jnp.concatenate(lows_i, axis=0).astype(BF16)
        low_d = jnp.concatenate(lows_d, axis=0).astype(BF16)
        st = jnp.concatenate(hids, axis=0).astype(BF16)
        states_v[:, sl] = dot(permt_s[...], st).astype(BF16)
        turn = ((1,), (1,))
        ig = jnp.concatenate(direct, axis=0) + dot(low_i, wi_v[h], turn) + dot(low_d, wd_v[h], turn)
        grads_v[:, sl] = dot(permt_s[...], ig.astype(BF16)).astype(BF16)
        both = jnp.concatenate([low_i, low_d], axis=1)
        wg = dot(actp[h], both, ((0,), (0,)))
        part[2 * h] = wg[:ROWS]
        part[2 * h + 1] = wg[ROWS:]
        sums = tile_of(
            [jnp.sum(s, axis=0, keepdims=True) for s in (sum_i, sum_d, sum_l)]
        )
        for half in range(2):
            to = 2 * h + half
            piece = sums[:, half * ROWS : (half + 1) * ROWS]
            bias_send[to] = piece

            @pl.when(to == me)
            def _():
                bias_recv[me] = piece

            send_tile(bias_send, bias_recv, small_sem.at[4], small_sem.at[5], to)
        return carry

    lax.fori_loop(0, HEADS, phase_b, 0)
    stores = [
        pltpu.make_async_copy(states_v, states_hbm, out_sem.at[0]),
        pltpu.make_async_copy(grads_v, grads_hbm, out_sem.at[1]),
    ]
    for c in stores:
        c.start()

    def gcols(g):
        return slice(g * BW, (g + 1) * BW)

    def z_at(off):
        return lax.rem(z + off + RING_Z, RING_Z)

    def y_at(off):
        return lax.rem(y + off + RING_Y, RING_Y)

    sends = []

    def launch(src, dst, ssem, rsem, ty, tz):
        copy = pltpu.make_async_remote_copy(
            src_ref=src,
            dst_ref=dst,
            send_sem=ssem,
            recv_sem=rsem,
            device_id={"seq": ty * RING_Z + tz},
            device_id_type=MESH,
        )
        copy.start()
        sends.append(copy)
        return copy

    z1, y1, z2, y2 = {}, {}, {}, {}

    def z1_send(c, i):
        g, way, hops = Z_CHAINS[c]
        n = Z_SLOT[(c, i)]
        zd = z_at(way * (hops - i))
        if i:
            z1[(c, i - 1)].wait_recv()
        for yd in range(RING_Y):
            v = part[yd * RING_Z + zd, 0:ROWS_ZY, gcols(g)]
            if i:
                v = v + z1r[n - 1, yd].astype(F32)
            z1s[n, yd] = v.astype(BF16)
        z1[(c, i)] = launch(z1s.at[n], z1r.at[n], z1_ss.at[n], z1_rs.at[n], y, z_at(way))

    def z1_fin():
        for c, (g, way, hops) in enumerate(Z_CHAINS):
            z1[(c, hops - 1)].wait_recv()
        for g in range(2):
            ns = [Z_SLOT[(c, ch[2] - 1)] for c, ch in enumerate(Z_CHAINS) if ch[0] == g]
            for yd in range(RING_Y):
                at = yd * RING_Z + z
                part[at, 0:ROWS_ZY, gcols(g)] = part[at, 0:ROWS_ZY, gcols(g)] + (
                    z1r[ns[0], yd].astype(F32) + z1r[ns[1], yd].astype(F32)
                )

    def y1_send(c, i, j):
        g, way, hops = Y_CHAINS[c]
        n = Y_SLOT[(c, i)]
        yd = y_at(way * (hops - i))
        if i:
            y1[(c, i - 1, j)].wait_recv()
        for q, off in enumerate(Z_SUBS[j]):
            v = part[yd * RING_Z + z_at(off), ROWS_ZY:ROWS, gcols(g)]
            if i:
                v = v + y1r[n - 1, j, q].astype(F32)
            y1s[n, j, q] = v.astype(BF16)
        y1[(c, i, j)] = launch(
            y1s.at[n, j], y1r.at[n, j], y1_ss.at[n, j], y1_rs.at[n, j], y_at(way), z
        )

    def y1_init(j):
        for c in (0, 3, 2, 1):
            y1_send(c, 0, j)

    def y1_forward(j):
        for c in (0, 3):
            y1_send(c, 1, j)

    def y1_fin(j):
        for c, (g, way, hops) in enumerate(Y_CHAINS):
            y1[(c, hops - 1, j)].wait_recv()
        for g in range(2):
            ns = [Y_SLOT[(c, ch[2] - 1)] for c, ch in enumerate(Y_CHAINS) if ch[0] == g]
            for q, off in enumerate(Z_SUBS[j]):
                at = y * RING_Z + z_at(off)
                part[at, ROWS_ZY:ROWS, gcols(g)] = part[at, ROWS_ZY:ROWS, gcols(g)] + (
                    y1r[ns[0], j, q].astype(F32) + y1r[ns[1], j, q].astype(F32)
                )

    def z2_step(distance):
        for c, (g, way, hops) in enumerate(Z_CHAINS):
            i = hops - distance
            if i < 0:
                continue
            n = Z_SLOT[(c, i)]
            if i:
                z2[(c, i - 1)].wait_recv()
            v = part[y * RING_Z + z_at(way * distance), ROWS_ZY:ROWS, gcols(g)]
            if i:
                v = v + z2r[n - 1].astype(F32)
            z2s[n] = v.astype(BF16)
            z2[(c, i)] = launch(z2s.at[n], z2r.at[n], z2_ss.at[n], z2_rs.at[n], y, z_at(way))

    def y2_step(distance):
        for c, (g, way, hops) in enumerate(Y_CHAINS):
            i = hops - distance
            if i < 0:
                continue
            n = Y_SLOT[(c, i)]
            if i:
                y2[(c, i - 1)].wait_recv()
            v = part[y_at(way * distance) * RING_Z + z, 0:ROWS_ZY, gcols(g)]
            if i:
                v = v + y2r[n - 1].astype(F32)
            y2s[n] = v.astype(BF16)
            y2[(c, i)] = launch(y2s.at[n], y2r.at[n], y2_ss.at[n], y2_rs.at[n], y_at(way), z)

    y1_init(0)
    for c in range(4):
        z1_send(c, 0)
    y1_init(1)
    y1_forward(0)
    y1_init(2)
    for c in range(4):
        z1_send(c, 1)
    y1_forward(1)
    y1_init(3)
    y1_fin(0)
    z2_step(4)
    for c in range(4):
        z1_send(c, 2)
    y1_forward(2)
    y1_fin(1)
    z2_step(3)
    for c in (0, 3):
        z1_send(c, 3)
    y1_forward(3)
    y1_fin(2)
    z2_step(2)
    z1_fin()
    y2_step(2)
    y2_step(1)
    y1_fin(3)
    z2_step(1)

    wait_tiles(bias_recv, small_sem.at[5])
    total = bias_recv[0]
    for s in range(1, SEQ_DEVICES):
        total = total + bias_recv[s]
    mine = logit_ref[:, pl.ds(pl.multiple_of(me * ROWS, ROWS), ROWS)]
    vec_ref[0:1, :] = total[0:1]
    vec_ref[1:2, :] = total[1:2]
    vec_ref[2:3, :] = total[2:3] * (-DECAY_SCALE / (1.0 + jnp.exp(-mine)))

    outs = (wgi_ref, wgd_ref)
    for c, (g, way, hops) in enumerate(Y_CHAINS):
        y2[(c, hops - 1)].wait_recv()
    for c, (g, way, hops) in enumerate(Z_CHAINS):
        z2[(c, hops - 1)].wait_recv()
    for g in range(2):
        ny = [Y_SLOT[(c, ch[2] - 1)] for c, ch in enumerate(Y_CHAINS) if ch[0] == g]
        nz = [Z_SLOT[(c, ch[2] - 1)] for c, ch in enumerate(Z_CHAINS) if ch[0] == g]
        outs[g][0:ROWS_ZY, :] = part[me, 0:ROWS_ZY, gcols(g)] + (
            y2r[ny[0]].astype(F32) + y2r[ny[1]].astype(F32)
        )
        outs[g][ROWS_ZY:ROWS, :] = part[me, ROWS_ZY:ROWS, gcols(g)] + (
            z2r[nz[0]].astype(F32) + z2r[nz[1]].astype(F32)
        )

    for s in sends:
        s.wait_send()
    wait_tiles(map_send, small_sem.at[0])
    wait_tiles(rep_send, small_sem.at[2])
    wait_tiles(bias_send, small_sem.at[4])
    for c in stores:
        c.wait()


def on_device(act, wi, wd, bi, bd, logits, docs, cot):
    any_spec = pl.BlockSpec(memory_space=pl.ANY)
    vmem = pl.BlockSpec(memory_space=pltpu.VMEM)
    smem = pl.BlockSpec(memory_space=pltpu.SMEM)
    chunk = (HEADS, ROWS, BW)
    scratch = [
        pltpu.VMEM((ROWS, WIDTH), BF16),
        pltpu.VMEM((ROWS, WIDTH), BF16),
        pltpu.VMEM((HEADS, BW, BW), BF16),
        pltpu.VMEM((HEADS, BW, BW), BF16),
        pltpu.VMEM(chunk, BF16),
        pltpu.VMEM(chunk, F32),
        pltpu.VMEM(chunk, F32),
        pltpu.VMEM(chunk, F32),
        pltpu.VMEM(chunk, F32),
        pltpu.VMEM(chunk, F32),
        pltpu.VMEM(chunk, F32),
        pltpu.VMEM(chunk, F32),
        pltpu.VMEM((ROWS, BW), F32),
        pltpu.VMEM((ROWS, BW), F32),
        pltpu.VMEM((1, WIDTH), F32),
        pltpu.VMEM((ROWS, ROWS), BF16),
        pltpu.VMEM((ROWS, ROWS), BF16),
        pltpu.VMEM((HEADS, 4, 8, BW), F32),
        pltpu.VMEM((ROWS, WIDTH), BF16),
        pltpu.VMEM((ROWS, WIDTH), BF16),
        pltpu.VMEM((SEQ_DEVICES, ROWS, 2 * BW), F32),
    ]
    scratch += [pltpu.VMEM((SEQ_DEVICES, 8, ROWS), F32) for _ in range(6)]
    for shape in (
        (Z_COUNT, RING_Y, ROWS_ZY, BW),
        (Y_COUNT, 4, 2, ROWS_YZ, BW),
        (Z_COUNT, ROWS_YZ, BW),
        (Y_COUNT, ROWS_ZY, BW),
    ):
        scratch += [pltpu.VMEM(shape, BF16), pltpu.VMEM(shape, BF16)]
    scratch += [
        pltpu.SemaphoreType.DMA((GROUPS, 4)),
        pltpu.SemaphoreType.DMA((2,)),
        pltpu.SemaphoreType.DMA((6,)),
    ]
    for shape in ((Z_COUNT,), (Y_COUNT, 4), (Z_COUNT,), (Y_COUNT,)):
        scratch += [pltpu.SemaphoreType.DMA(shape), pltpu.SemaphoreType.DMA(shape)]
    states, grads, wgi, wgd, vec = pl.pallas_call(
        kernel,
        out_shape=(
            jax.ShapeDtypeStruct((ROWS, WIDTH), BF16),
            jax.ShapeDtypeStruct((ROWS, WIDTH), BF16),
            jax.ShapeDtypeStruct((ROWS, BW), F32),
            jax.ShapeDtypeStruct((ROWS, BW), F32),
            jax.ShapeDtypeStruct((8, ROWS), F32),
        ),
        in_specs=[smem, any_spec, any_spec, any_spec, vmem, vmem, vmem, any_spec],
        out_specs=(any_spec, any_spec, vmem, vmem, vmem),
        scratch_shapes=scratch,
        compiler_params=pltpu.CompilerParams(
            collective_id=0, has_side_effects=True, vmem_limit_bytes=60 * 1024 * 1024
        ),
    )(
        docs,
        act,
        wi,
        wd,
        bi.reshape(1, WIDTH),
        bd.reshape(1, WIDTH),
        logits.reshape(1, WIDTH),
        cot,
    )
    return states, grads, wgi, wgd, vec[0], vec[1], vec[2]


def solution(mesh):
    rows = P(("grp", "seq"), None)
    flat = P(("grp", "seq"))
    return jax.shard_map(
        on_device,
        mesh=mesh,
        in_specs=(rows, P(), P(), P(), P(), P(), P("grp"), rows),
        out_specs=(rows, rows, rows, rows, flat, flat, flat),
        check_vma=False,
    )
```

time: 1010 us -> 80.7 us (0.08)
  blocking collectives: 337 us -> 0 us
  local copies, waits for them, and re-layouts: 290 us -> 5.94 us
  waiting for transfers between devices: 269 us -> 0 us
  Pallas kernels: 0 us -> 73.9 us
  other arithmetic: 70.3 us -> 0 us
  matrix products: 18.4 us -> 0 us
  between operations: 15.1 us -> 0.66 us
    reduce_scatter x2 -> x0, waiting for transfers between devices: 269 us -> none  [the longest x1 224 us: on_device(): lax.psum_scatter(term_decay, 'seq', scatter_dimension=0, tiled=True)]
    all_gather x4 -> x0, blocking collectives: 197 us -> none  [carried_in(): everything = jax.tree.map(lambda part: lax.all_gather(part, axis), x)]
    unnamed x1 -> x0, blocking collectives: 141 us -> none
    another operation x36 -> x0, local copies, waits for them, and re-layouts: 84.7 us -> none  [the longest x16 45.9 us: advance(): jnp.stack(prods, axis=0)]
    slice x33 -> x0, local copies, waits for them, and re-layouts: 74.8 us -> none  [the longest x16 37.4 us: advance(): running_prod = fac_block[place] * running_prod]
    pallas_call x0 -> x1, Pallas kernels: none -> 73.9 us  [on_device(): pl.pallas_call(kernel, out_shape=(jax.ShapeDtypeStruct((ROWS, WIDTH), BF1...]
    dynamic_slice x64 -> x0, local copies, waits for them, and re-layouts: 63.8 us -> none  [hop(): new = combine(before, jax.tree.map(lambda part: part[at], everything))]
    dynamic_update_slice x16 -> x0, local copies, waits for them, and re-layouts: 28.7 us -> none  [local_chain(): lax.scan(advance, start, (fac3, val3), reverse=reverse)]
  transfers between devices with their start and end apart: 2 -> 0, of which waited for: 2 -> 0; matrix products, arithmetic and copies ran while one was open for 3% -> 0% of each run, Pallas kernels for 0% -> 0%
where the time goes in v1:
time: 80.7 us; the launch traced here: 80.5 us
  Pallas kernels  73.9 us (92%)
  local copies, waits for them, and re-layouts  5.94 us (7%)
    pallas_call x1, Pallas kernels, on_device(): pl.pallas_call(kernel, out_shape=(jax.ShapeDtypeStruct((ROWS, WIDTH), BF1...  73.9 us
    unnamed x10, local copies, waits for them, and re-layouts  4.62 us

profile of v1, /device:TPU:2, one launch (start us, length us, event | category | flops | bytes accessed | tf_op | source)
XLA Modules:
  0.0 80.5 jit_solution(3459775066364555464)
XLA Ops:
  0.6 73.9 %shard_map.135 = (bf16[128,4096]{1,0:T(8,128)(2,1)}, bf16[128,4096]{1,0:T(8,128)(2,1)}, f32[128,256]{1,0:T(8,128)}, f32[128,256]{1,0:T(8,128)}, f32[8,128]{1,0:T(8,128)}) custom-call(s32[6]{0:T(128)} %docs_ref.1, bf16[128,4096]{1,0:T(8,128)(2,1)} %act_hbm.1, bf16[16,256,256]{2,1,0:T(8,128)(2,1)} %wi_hbm.1, bf16[16,256,256]{2,1,0:T(8,128)(2,1)} %wd_hbm.1, ...), custom_call_target="tpu_custom_call" | custom-call | tf_op jit(solution)/shard_map/pallas_call | solution.py:562
  74.5 0.0 copy-start
  74.5 1.3 %slice_bitcast_fusion = (f32[128]{0:T(128)}, f32[128]{0:T(128)}, f32[128]{0:T(128)}) fusion(f32[8,128]{1,0:T(8,128)} %get-tuple-element.16), kind=kLoop, calls=%fused_computation | loop fusion | bytes 3072 | tf_op jit(solution)/shard_map/squeeze | solution.py:587
  75.8 0.0 copy-start.2
  75.8 0.0 copy-start.1
  75.8 2.3 %copy.19 = bf16[128,4096]{1,0:T(8,128)(2,1)} copy(bf16[128,4096]{1,0:T(8,128)(2,1)} %get-tuple-element.27) | data formatting | bytes 2097152
  78.2 0.0 copy-done
  78.2 1.0 %copy.20 = bf16[128,4096]{1,0:T(8,128)(2,1)} copy(bf16[128,4096]{1,0:T(8,128)(2,1)S(1)} %copy-done) | data formatting | bytes 2097152
  79.1 0.0 copy-done.2
  79.1 0.7 copy.21
  79.8 0.0 copy-done.1
  79.8 0.7 copy.22
Async XLA Ops:
  74.5 3.7 %copy-start = (bf16[128,4096]{1,0:T(8,128)(2,1)S(1)}, bf16[128,4096]{1,0:T(8,128)(2,1)}, u32[]{:S(2)}) copy-start(bf16[128,4096]{1,0:T(8,128)(2,1)} %get-tuple-element.28) | copy-start | bytes 3145732
  75.8 3.3 %copy-start.2 = (f32[128,256]{1,0:T(8,128)S(1)}, f32[128,256]{1,0:T(8,128)}, u32[]{:S(2)}) copy-start(f32[128,256]{1,0:T(8,128)} %get-tuple-element.29) | copy-start | bytes 393220
  75.8 4.0 %copy-start.1 = (f32[128,256]{1,0:T(8,128)S(1)}, f32[128,256]{1,0:T(8,128)}, u32[]{:S(2)}) copy-start(f32[128,256]{1,0:T(8,128)} %get-tuple-element.30) | copy-start | bytes 393220

commit v2 on v1

v2 whole, which is shorter than its diff:
```python
import jax
import jax.numpy as jnp
from jax import lax
from jax.experimental import pallas as pl
from jax.experimental.pallas import tpu as pltpu
from jax.sharding import PartitionSpec as P

ROWS = 128
WIDTH = 4096
HEADS = 16
BW = 256
DOCS = 6
RING_Y = 4
RING_Z = 8
SEQ_DEVICES = RING_Y * RING_Z
STEPS = 16
GROUPS = 4
ZY = 128
YZ = 2 * BW - ZY
HALF = ROWS // 2
DECAY_SCALE = 8.0
ROOT_LIMIT = 2000.0
TINY = 1.2e-38
MESH = pl.DeviceIdType.MESH
F32 = jnp.float32
BF16 = jnp.bfloat16

Z_CHAINS = ((0, 1, 4), (0, -1, 3), (1, 1, 3), (1, -1, 4))
LOG2E = 1.4426950408889634
LN2 = 0.6931471805599453
RESET = -1e4


def slots_of(chains):
    table, count = {}, 0
    for c, (_, _, hops) in enumerate(chains):
        for i in range(hops):
            table[(c, i)] = count
            count += 1
    return table, count


Z_SLOT, Z_COUNT = slots_of(Z_CHAINS)


def dot(a, b, dims=((1,), (0,))):
    return lax.dot_general(a, b, (dims, ((), ())), preferred_element_type=F32)


def recip(x):
    return pltpu.reciprocal(x, approx=True)


def tile_of(rows):
    pad = jnp.zeros((8 - len(rows), rows[0].shape[1]), F32)
    return jnp.concatenate(list(rows) + [pad], axis=0)


def kernel(
    docs_ref,
    act_hbm,
    wi_hbm,
    wd_hbm,
    bi_ref,
    bd_ref,
    logit_ref,
    cot_hbm,
    states_hbm,
    grads_hbm,
    wgi_ref,
    wgd_ref,
    vec_ref,
    act_v,
    cot_v,
    w_v,
    actp,
    cotp,
    fac,
    psh,
    coef,
    quo,
    gin,
    dgate,
    low_s,
    st_s,
    u_s,
    reset_s,
    k8_s,
    perm_s,
    permt_s,
    seg_s,
    states_v,
    grads_v,
    part,
    prods,
    pair_a,
    pair_b,
    gates_a,
    gates_b,
    act_all,
    low_all,
    map_send,
    map_recv,
    rep_send,
    rep_recv,
    bias_send,
    bias_recv,
    z1s,
    z1r,
    z2s,
    z2r,
    y2s,
    y2r,
    in_sem,
    out_sem,
    small_sem,
    z1_ss,
    z1_rs,
    z2_ss,
    z2_rs,
    y2_ss,
    y2_rs,
    act_ss,
    act_rs,
    low_ss,
    low_rs,
):
    me = lax.axis_index("seq")
    y, z = me // RING_Z, lax.rem(me, RING_Z)

    gw = WIDTH // GROUPS
    gh = HEADS // GROUPS

    def fetch(g):
        cols = pl.ds(pl.multiple_of(g * gw, gw), gw)
        heads = pl.ds(g * gh, gh)
        pairs = (
            (act_hbm.at[:, cols], act_v.at[:, cols]),
            (wi_hbm.at[heads], w_v.at[heads, :, 0:BW]),
            (wd_hbm.at[heads], w_v.at[heads, :, BW:]),
            (cot_hbm.at[:, cols], cot_v.at[:, cols]),
        )
        return [pltpu.make_async_copy(s, d, in_sem.at[g, i]) for i, (s, d) in enumerate(pairs)]

    for g in range(GROUPS):
        for c in fetch(g):
            c.start()

    barrier = pltpu.get_barrier_semaphore()

    def hello(i, carry):
        pl.semaphore_signal(
            barrier,
            inc=1,
            device_id={"seq": lax.rem(me + i, SEQ_DEVICES)},
            device_id_type=MESH,
        )
        return carry

    lax.fori_loop(1, SEQ_DEVICES, hello, 0)

    row = lax.broadcasted_iota(jnp.int32, (ROWS, ROWS), 0)
    col = lax.broadcasted_iota(jnp.int32, (ROWS, ROWS), 1)
    perm_s[...] = (col == (row & 7) * STEPS + (row >> 3)).astype(F32).astype(BF16)
    permt_s[...] = (row == (col & 7) * STEPS + (col >> 3)).astype(F32).astype(BF16)
    seg = lax.broadcasted_iota(jnp.int32, (8, BW), 0)
    first = me * ROWS + seg * STEPS
    starts = [jnp.int32(0)]
    for j in range(DOCS - 1):
        starts.append(starts[-1] + docs_ref[j])
    for k in range(STEPS):
        hit = first + k == starts[0]
        for j in range(1, DOCS):
            hit = hit | (first + k == starts[j])
        reset_s[8 * k : 8 * k + 8, :] = jnp.where(hit, RESET, 0.0)
    logits = logit_ref[...]
    e = jnp.exp(-jnp.abs(logits))
    series = e * (1.0 + e * (-1 / 2 + e * (1 / 3 + e * (-1 / 4 + e * (1 / 5 + e * (-1 / 6))))))
    soft = jnp.maximum(logits, 0.0) + jnp.where(e < 0.0625, series, jnp.log(1.0 + e))
    k8_s[...] = -DECAY_SCALE * soft

    def send_tile(src, dst, send_sem, recv_sem, to):
        @pl.when(to != me)
        def _():
            pltpu.make_async_remote_copy(
                src_ref=src.at[to],
                dst_ref=dst.at[me],
                send_sem=send_sem,
                recv_sem=recv_sem,
                device_id={"seq": to},
                device_id_type=MESH,
            ).start()

    def wait_tiles(buf, sem, n=8):
        view = buf.at[pl.ds(0, SEQ_DEVICES - 1), 0:n]
        pltpu.make_async_copy(view, view, sem).wait()

    def lanes(h):
        return pl.ds(pl.multiple_of(h * BW, BW), BW)

    def gate_dots(h, pair_s, gates_s):
        sl = lanes(h)

        @pl.when(lax.rem(h, gh) == 0)
        def _():
            for c in fetch(h // gh):
                c.wait()

        pair = dot(perm_s[...], jnp.concatenate([act_v[:, sl], cot_v[:, sl]], axis=1))
        pair_s[...] = pair
        xb = pair[:, :BW].astype(BF16)
        actp[h] = xb
        gates_s[...] = dot(xb, w_v[h])

    def local_maps(h, pair_s, gates_s):
        sl = lanes(h)
        bi, bd = bi_ref[:, sl], bd_ref[:, sl]
        k8 = k8_s[:, sl] * LOG2E
        prod = jnp.ones((8, BW), F32)
        fwd = jnp.zeros((8, BW), F32)
        bwd = jnp.zeros((8, BW), F32)
        for k in range(STEPS):
            r = slice(8 * k, 8 * k + 8)
            xk = pair_s[r, :BW]
            ct = pair_s[r, BW:]
            cotp[h, r, :] = ct
            ig = recip(1.0 + jnp.exp2((gates_s[r, :BW] + bi) * -LOG2E))
            dg = recip(1.0 + jnp.exp2((gates_s[r, BW:] + bd) * -LOG2E))
            ld = dg * k8 + reset_s[r, :]
            f = jnp.exp2(ld)
            th = jnp.tanh(ld * -LN2)
            comp = th + th * (f * f)
            root = lax.rsqrt(jnp.maximum(comp, TINY))
            a = ig * (comp * root)
            p = xk * a
            fac[h, r, :] = f
            psh[h, r, :] = p
            coef[h, r, :] = a
            quo[h, r, :] = f * (xk * ig) * jnp.minimum(root, ROOT_LIMIT)
            gin[h, r, :] = p * (1.0 - ig)
            dgate[h, r, :] = dg
            fwd = f * fwd + p
            prod = prod * f
            bwd = bwd + prod * ct
        fa, ba = prod, prod
        for d in (1, 2, 4):
            later = seg >= d
            fwd = jnp.where(later, fa * pltpu.roll(fwd, d, 0) + fwd, fwd)
            fa = jnp.where(later, fa * pltpu.roll(fa, d, 0), fa)
            earlier = seg < 8 - d
            bwd = jnp.where(earlier, ba * pltpu.roll(bwd, 8 - d, 0) + bwd, bwd)
            ba = jnp.where(earlier, ba * pltpu.roll(ba, 8 - d, 0), ba)
        whole = tile_of((fa[7:8], fwd[7:8], bwd[0:1]))
        seg_s[h, 0] = jnp.where(seg == 0, 1.0, pltpu.roll(fa, 1, 0))
        seg_s[h, 1] = jnp.where(seg == 0, 0.0, pltpu.roll(fwd, 1, 0))
        seg_s[h, 2] = jnp.where(seg == 7, 1.0, pltpu.roll(ba, 7, 0))
        seg_s[h, 3] = jnp.where(seg == 7, 0.0, pltpu.roll(bwd, 7, 0))
        for half in range(2):
            map_send[2 * h + half] = whole[:, half * ROWS : (half + 1) * ROWS]

    def share(h):
        for half in range(2):
            to = 2 * h + half

            @pl.when(to == me)
            def _():
                map_recv[me] = map_send[me]

            send_tile(map_send, map_recv, small_sem.at[0], small_sem.at[1], to)
        yd, q = h // (RING_Z // 2), lax.rem(h, RING_Z // 2)
        d = lax.rem(yd - y + RING_Y, RING_Y)

        @pl.when(d == 0)
        def _():
            act_all[q, 0] = actp[h]

        @pl.when(d != 0)
        def _():
            pltpu.make_async_remote_copy(
                src_ref=actp.at[h],
                dst_ref=act_all.at[q, d],
                send_sem=act_ss.at[q, d],
                recv_sem=act_rs.at[q, d],
                device_id={"seq": yd * RING_Z + z},
                device_id_type=MESH,
            ).start()

    def two_heads(i, carry):
        gate_dots(2 * i + 1, pair_b, gates_b)
        local_maps(2 * i, pair_a, gates_a)
        gate_dots(2 * i + 2 - (2 * i + 2) // HEADS, pair_a, gates_a)
        local_maps(2 * i + 1, pair_b, gates_b)
        return carry

    def two_heads_and_share(i, carry):
        two_heads(i, carry)
        for k in range(2):
            share(2 * i + k - HEADS // 2)
            share(2 * i + k)
        return carry

    gate_dots(0, pair_a, gates_a)
    lax.fori_loop(0, HEADS // 4, two_heads, 0)
    pl.semaphore_wait(barrier, SEQ_DEVICES - 1)
    lax.fori_loop(HEADS // 4, HEADS // 2, two_heads_and_share, 0)

    wait_tiles(map_recv, small_sem.at[1])
    hid = jnp.zeros((1, ROWS), F32)
    for s in range(SEQ_DEVICES):
        rep_send[s, 0:1, :] = hid
        hid = map_recv[s, 0:1, :] * hid + map_recv[s, 1:2, :]
    back = jnp.zeros((1, ROWS), F32)
    for s in reversed(range(SEQ_DEVICES)):
        rep_send[s, 1:2, :] = back
        back = map_recv[s, 0:1, :] * back + map_recv[s, 2:3, :]
    rep_recv[me, 0:2] = rep_send[me, 0:2]

    def reply(i, carry):
        to = lax.rem(me + i, SEQ_DEVICES)
        pltpu.make_async_remote_copy(
            src_ref=rep_send.at[to, 0:2],
            dst_ref=rep_recv.at[me, 0:2],
            send_sem=small_sem.at[2],
            recv_sem=small_sem.at[3],
            device_id={"seq": to},
            device_id_type=MESH,
        ).start()
        return carry

    lax.fori_loop(1, SEQ_DEVICES, reply, 0)
    wait_tiles(rep_recv, small_sem.at[3], 2)

    def chains(h):
        sl = lanes(h)
        t0, t1 = rep_recv[2 * h], rep_recv[2 * h + 1]
        hin = jnp.concatenate([t0[0:1], t1[0:1]], axis=1)
        cin = jnp.concatenate([t0[1:2], t1[1:2]], axis=1)
        hid = seg_s[h, 0] * hin + seg_s[h, 1]
        c = seg_s[h, 2] * cin + seg_s[h, 3]
        for k in reversed(range(STEPS)):
            r = slice(8 * k, 8 * k + 8)
            u = cotp[h, r, :] + c
            u_s[r, :] = u
            c = fac[h, r, :] * u
        k8 = k8_s[:, sl]
        sum_i = jnp.zeros((8, BW), F32)
        sum_d = jnp.zeros((8, BW), F32)
        sum_l = jnp.zeros((8, BW), F32)
        hids, lows_i, lows_d = [], [], []
        for k in range(STEPS):
            r = slice(8 * k, 8 * k + 8)
            u = u_s[r, :]
            f = fac[h, r, :]
            dg = dgate[h, r, :]
            dl = f * u * (hid - quo[h, r, :]) * dg
            pd = k8 * dl * (1.0 - dg)
            pi = u * gin[h, r, :]
            hid = f * hid + psh[h, r, :]
            sum_i = sum_i + pi
            sum_d = sum_d + pd
            sum_l = sum_l + dl
            hids.append(hid)
            lows_i.append(pi)
            lows_d.append(pd)
            coef[h, r, :] = u * coef[h, r, :]
        low_i = jnp.concatenate(lows_i, axis=0).astype(BF16)
        low_d = jnp.concatenate(lows_d, axis=0).astype(BF16)
        st_s[h] = jnp.concatenate(hids, axis=0).astype(BF16)
        both = jnp.concatenate([low_i, low_d], axis=1)
        low_s[h] = both
        wg = dot(actp[h], both[:, YZ:], ((0,), (0,)))
        part[2 * h] = wg[:ROWS]
        part[2 * h + 1] = wg[ROWS:]
        sums = tile_of(
            [jnp.sum(s, axis=0, keepdims=True) for s in (sum_i, sum_d, sum_l)]
        )
        for half in range(2):
            to = 2 * h + half
            piece = sums[:, half * ROWS : (half + 1) * ROWS]
            bias_send[to] = piece

            @pl.when(to == me)
            def _():
                bias_recv[me] = piece

            send_tile(bias_send, bias_recv, small_sem.at[4], small_sem.at[5], to)

    zp, odd = z // 2, lax.rem(z, 2)

    def group_of(j):
        return lax.rem(zp + (2, 1 + 2 * odd, 3 - 2 * odd, 0)[j], RING_Z // 2)

    def make_group(j):
        q = group_of(j)

        def one(i, carry):
            d = lax.rem(i + 2, RING_Y)
            yd = lax.rem(y + d, RING_Y)
            h = yd * (RING_Z // 2) + q
            chains(h)

            @pl.when(d == 0)
            def _():
                low_all[q, 0] = low_s[h, :, :YZ]

            @pl.when(d != 0)
            def _():
                pltpu.make_async_remote_copy(
                    src_ref=low_s.at[h, :, pl.ds(0, YZ)],
                    dst_ref=low_all.at[q, d],
                    send_sem=low_ss.at[j, d],
                    recv_sem=low_rs.at[j, d],
                    device_id={"seq": yd * RING_Z + z},
                    device_id_type=MESH,
                ).start()

            return carry

        lax.fori_loop(0, RING_Y, one, 0)

    def finish(h, carry):
        sl = lanes(h)
        ig = coef[h] + dot(low_s[h], w_v[h], ((1,), (1,)))
        out = dot(permt_s[...], jnp.concatenate([st_s[h], ig.astype(BF16)], axis=1)).astype(BF16)
        states_v[:, sl] = out[:, :BW]
        grads_v[:, sl] = out[:, BW:]
        return carry

    def finish_quarter(i):
        lax.fori_loop(i * HEADS // 4, (i + 1) * HEADS // 4, finish, 0)

    def half(p):
        return slice(p * HALF, (p + 1) * HALF)

    def landed(buf, sem):
        pltpu.make_async_copy(buf, buf, sem).wait()

    def z_at(off):
        return lax.rem(z + off + RING_Z, RING_Z)

    def y_at(off):
        return lax.rem(y + off + RING_Y, RING_Y)

    sends = []

    def launch(src, dst, ssem, rsem, ty, tz):
        copy = pltpu.make_async_remote_copy(
            src_ref=src,
            dst_ref=dst,
            send_sem=ssem,
            recv_sem=rsem,
            device_id={"seq": ty * RING_Z + tz},
            device_id_type=MESH,
        )
        copy.start()
        sends.append(copy)
        return copy

    z1, z2, y2 = {}, {}, {}

    def z1_send(c, i):
        p, way, hops = Z_CHAINS[c]
        n = Z_SLOT[(c, i)]
        zd = z_at(way * (hops - i))
        if i:
            z1[(c, i - 1)].wait_recv()
        for d in range(RING_Y):
            v = part[y_at(d) * RING_Z + zd, half(p), :]
            if i:
                v = v + z1r[n - 1, d].astype(F32)
            z1s[n, d] = v.astype(BF16)
        z1[(c, i)] = launch(z1s.at[n], z1r.at[n], z1_ss.at[n], z1_rs.at[n], y, z_at(way))

    def last_of(p):
        return [Z_SLOT[(c, ch[2] - 1)] for c, ch in enumerate(Z_CHAINS) if ch[0] == p]

    def z1_fin():
        for c, (p, way, hops) in enumerate(Z_CHAINS):
            z1[(c, hops - 1)].wait_recv()
        for p in range(2):
            n, m = last_of(p)
            for d in range(RING_Y):
                v = part[y_at(d) * RING_Z + z, half(p), :] + (
                    z1r[n, d].astype(F32) + z1r[m, d].astype(F32)
                )
                if d:
                    y2s[d, half(p), :] = v.astype(BF16)
                else:
                    part[me, half(p), :] = v
        for d in (2, 1, 3):
            y2[d] = launch(y2s.at[d], y2r.at[d], y2_ss.at[d], y2_rs.at[d], y_at(d), z)

    def product(j):
        q = group_of(j)
        for d in range(1, RING_Y):
            if j == 0:
                for k in range(RING_Z // 2):
                    landed(act_all.at[k, d], act_rs.at[k, d])
            landed(low_all.at[q, d], low_rs.at[j, d])
        acts = act_all[q].reshape(RING_Y * ROWS, BW)
        lows = low_all[q].reshape(RING_Y * ROWS, YZ)
        wg = dot(acts, lows, ((0,), (0,)))
        prods[2 * q] = wg[:ROWS]
        prods[2 * q + 1] = wg[ROWS:]

    def z2_step(distance):
        for c, (p, way, hops) in enumerate(Z_CHAINS):
            i = hops - distance
            if i < 0:
                continue
            n = Z_SLOT[(c, i)]
            if i:
                z2[(c, i - 1)].wait_recv()
            v = prods[z_at(way * distance), half(p), :]
            if i:
                v = v + z2r[n - 1].astype(F32)
            z2s[n] = v.astype(BF16)
            z2[(c, i)] = launch(z2s.at[n], z2r.at[n], z2_ss.at[n], z2_rs.at[n], y, z_at(way))

    def z1_sends(*which):
        for c, i in which:
            z1_send(c, i)

    make_group(0)
    z1_sends((0, 0), (3, 0))
    make_group(1)
    z1_sends((1, 0), (2, 0))
    make_group(2)
    z1_sends((0, 1), (3, 1))
    make_group(3)
    z1_sends((1, 1), (2, 1))
    product(0)
    z2_step(4)
    z1_sends((0, 2), (3, 2))
    finish_quarter(0)
    z1_sends((1, 2), (2, 2), (0, 3), (3, 3))
    product(1)
    z2_step(3)
    finish_quarter(1)
    z1_fin()
    finish_quarter(2)
    product(2)
    z2_step(2)
    finish_quarter(3)
    stores = [
        pltpu.make_async_copy(states_v, states_hbm, out_sem.at[0]),
        pltpu.make_async_copy(grads_v, grads_hbm, out_sem.at[1]),
    ]
    for c in stores:
        c.start()
    product(3)
    z2_step(1)

    wait_tiles(bias_recv, small_sem.at[5])
    total = bias_recv[0]
    for s in range(1, SEQ_DEVICES):
        total = total + bias_recv[s]
    mine = logit_ref[:, pl.ds(pl.multiple_of(me * ROWS, ROWS), ROWS)]
    vec_ref[0:1, :] = total[0:1]
    vec_ref[1:2, :] = total[1:2]
    vec_ref[2:3, :] = total[2:3] * (-DECAY_SCALE / (1.0 + jnp.exp(-mine)))

    for d in range(1, RING_Y):
        y2[d].wait_recv()
    rest = part[me] + (y2r[1].astype(F32) + y2r[2].astype(F32) + y2r[3].astype(F32))
    wgd_ref[:, 2 * BW - YZ :] = rest
    for c, (p, way, hops) in enumerate(Z_CHAINS):
        z2[(c, hops - 1)].wait_recv()
    for p in range(2):
        n, m = last_of(p)
        done = prods[z, half(p), :] + (z2r[n].astype(F32) + z2r[m].astype(F32))
        wgi_ref[half(p), :] = done[:, :BW]
        wgd_ref[half(p), : YZ - BW] = done[:, BW:]

    for s in sends:
        s.wait_send()
    for d in range(1, RING_Y):
        for k in range(RING_Z // 2):
            landed(act_all.at[k, d], act_ss.at[k, d])
            landed(low_all.at[k, d], low_ss.at[k, d])
    wait_tiles(map_send, small_sem.at[0])
    wait_tiles(rep_send, small_sem.at[2], 2)
    wait_tiles(bias_send, small_sem.at[4])
    for c in stores:
        c.wait()


def hand_over(*refs):
    ins, outs, sem = refs[:5], refs[5:12], refs[12]
    pairs = list(zip(ins[:4], outs[:4]))
    pairs += [(ins[4].at[pl.ds(i, 1)], outs[4 + i]) for i in range(3)]
    copies = [pltpu.make_async_copy(s, d, sem.at[i]) for i, (s, d) in enumerate(pairs)]
    for c in copies:
        c.start()
    for c in copies:
        c.wait()


def on_device(act, wi, wd, bi, bd, logits, docs, cot):
    any_spec = pl.BlockSpec(memory_space=pl.ANY)
    vmem = pl.BlockSpec(memory_space=pltpu.VMEM)
    smem = pl.BlockSpec(memory_space=pltpu.SMEM)
    chunk = (HEADS, ROWS, BW)
    scratch = [
        pltpu.VMEM((ROWS, WIDTH), BF16),
        pltpu.VMEM((ROWS, WIDTH), BF16),
        pltpu.VMEM((HEADS, BW, 2 * BW), BF16),
        pltpu.VMEM(chunk, BF16),
        pltpu.VMEM(chunk, F32),
        pltpu.VMEM(chunk, F32),
        pltpu.VMEM(chunk, F32),
        pltpu.VMEM(chunk, F32),
        pltpu.VMEM(chunk, F32),
        pltpu.VMEM(chunk, F32),
        pltpu.VMEM(chunk, F32),
        pltpu.VMEM((HEADS, ROWS, 2 * BW), BF16),
        pltpu.VMEM(chunk, BF16),
        pltpu.VMEM((ROWS, BW), F32),
        pltpu.VMEM((ROWS, BW), F32),
        pltpu.VMEM((1, WIDTH), F32),
        pltpu.VMEM((ROWS, ROWS), BF16),
        pltpu.VMEM((ROWS, ROWS), BF16),
        pltpu.VMEM((HEADS, 4, 8, BW), F32),
        pltpu.VMEM((ROWS, WIDTH), BF16),
        pltpu.VMEM((ROWS, WIDTH), BF16),
        pltpu.VMEM((SEQ_DEVICES, ROWS, ZY), F32),
        pltpu.VMEM((RING_Z, ROWS, YZ), F32),
        pltpu.VMEM((ROWS, 2 * BW), F32),
        pltpu.VMEM((ROWS, 2 * BW), F32),
        pltpu.VMEM((ROWS, 2 * BW), F32),
        pltpu.VMEM((ROWS, 2 * BW), F32),
        pltpu.VMEM((RING_Z // 2, RING_Y, ROWS, BW), BF16),
        pltpu.VMEM((RING_Z // 2, RING_Y, ROWS, YZ), BF16),
    ]
    scratch += [pltpu.VMEM((SEQ_DEVICES, 8, ROWS), F32) for _ in range(6)]
    for shape in (
        (Z_COUNT, RING_Y, HALF, ZY),
        (Z_COUNT, HALF, YZ),
        (RING_Y, ROWS, ZY),
    ):
        scratch += [pltpu.VMEM(shape, BF16), pltpu.VMEM(shape, BF16)]
    scratch += [
        pltpu.SemaphoreType.DMA((GROUPS, 4)),
        pltpu.SemaphoreType.DMA((2,)),
        pltpu.SemaphoreType.DMA((6,)),
    ]
    quads = (RING_Z // 2, RING_Y)
    for shape in ((Z_COUNT,), (Z_COUNT,), (RING_Y,), quads, quads):
        scratch += [pltpu.SemaphoreType.DMA(shape), pltpu.SemaphoreType.DMA(shape)]
    states, grads, wgi, wgd, vec = pl.pallas_call(
        kernel,
        out_shape=(
            jax.ShapeDtypeStruct((ROWS, WIDTH), BF16),
            jax.ShapeDtypeStruct((ROWS, WIDTH), BF16),
            jax.ShapeDtypeStruct((ROWS, BW), F32),
            jax.ShapeDtypeStruct((ROWS, BW), F32),
            jax.ShapeDtypeStruct((8, ROWS), F32),
        ),
        in_specs=[smem, any_spec, any_spec, any_spec, vmem, vmem, vmem, any_spec],
        out_specs=(any_spec, any_spec, vmem, vmem, vmem),
        scratch_shapes=scratch,
        compiler_params=pltpu.CompilerParams(
            collective_id=0, has_side_effects=True, vmem_limit_bytes=60 * 1024 * 1024
        ),
    )(
        docs,
        act,
        wi,
        wd,
        bi.reshape(1, WIDTH),
        bd.reshape(1, WIDTH),
        logits.reshape(1, WIDTH),
        cot,
    )
    outs = pl.pallas_call(
        hand_over,
        out_shape=[jax.ShapeDtypeStruct(a.shape, a.dtype) for a in (states, grads, wgi, wgd)]
        + [jax.ShapeDtypeStruct((1, ROWS), F32)] * 3,
        in_specs=[vmem] * 5,
        out_specs=[any_spec] * 7,
        scratch_shapes=[pltpu.SemaphoreType.DMA((7,))],
    )(states, grads, wgi, wgd, vec)
    return (*outs[:4], *(v.reshape(ROWS) for v in outs[4:]))


def solution(mesh):
    rows = P(("grp", "seq"), None)
    flat = P(("grp", "seq"))
    return jax.shard_map(
        on_device,
        mesh=mesh,
        in_specs=(rows, P(), P(), P(), P(), P(), P("grp"), rows),
        out_specs=(rows, rows, rows, rows, flat, flat, flat),
        check_vma=False,
    )
```

time: 80.7 us -> 65.5 us (0.81)
  Pallas kernels: 73.9 us -> 64.7 us
  local copies, waits for them, and re-layouts: 5.94 us -> 0 us
    pallas_call x1, Pallas kernels: 73.9 us -> 61.7 us  [on_device(): pl.pallas_call(kernel, out_shape=(jax.ShapeDtypeStruct((ROWS, WIDTH), BF1...]
    unnamed x10 -> x0, local copies, waits for them, and re-layouts: 4.62 us -> none
    pallas_call x0 -> x1, Pallas kernels: none -> 3.04 us  [on_device(): pl.pallas_call(hand_over, out_shape=[jax.ShapeDtypeStruct(a.shape, a.dtyp...]
    squeeze x1 -> x0, local copies, waits for them, and re-layouts: 1.32 us -> none  [on_device(): return (states, grads, wgi, wgd, vec[0], vec[1], vec[2])]
where the time goes in v2:
time: 65.5 us; the launch traced here: 65.3 us
  Pallas kernels  64.7 us (99%)
    pallas_call x1, Pallas kernels, on_device(): pl.pallas_call(kernel, out_shape=(jax.ShapeDtypeStruct((ROWS, WIDTH), BF1...  61.7 us
    pallas_call x1, Pallas kernels, on_device(): pl.pallas_call(hand_over, out_shape=[jax.ShapeDtypeStruct(a.shape, a.dtyp...  3.04 us

profile of v2, /device:TPU:2, one launch (start us, length us, event | category | flops | bytes accessed | tf_op | source)
XLA Modules:
  0.0 65.3 jit_solution(17914217838677200470)
XLA Ops:
  0.6 61.7 %shard_map.135 = (bf16[128,4096]{1,0:T(8,128)(2,1)}, bf16[128,4096]{1,0:T(8,128)(2,1)}, f32[128,256]{1,0:T(8,128)}, f32[128,256]{1,0:T(8,128)}, f32[8,128]{1,0:T(8,128)}) custom-call(s32[6]{0:T(128)} %docs_ref.1, bf16[128,4096]{1,0:T(8,128)(2,1)} %act_hbm.1, bf16[16,256,256]{2,1,0:T(8,128)(2,1)} %wi_hbm.1, bf16[16,256,256]{2,1,0:T(8,128)(2,1)} %wd_hbm.1, ...), custom_call_target="tpu_custom_call" | custom-call | tf_op jit(solution)/shard_map/pallas_call | solution.py:650
  62.3 3.0 %shard_map.136 = (bf16[128,4096]{1,0:T(8,128)(2,1)}, bf16[128,4096]{1,0:T(8,128)(2,1)}, f32[128,256]{1,0:T(8,128)}, f32[128,256]{1,0:T(8,128)}, f32[1,128]{1,0:T...) custom-call(bf16[128,4096]{1,0:T(8,128)(2,1)} %get-tuple-element.19.refs_0_, bf16[128,4096]{1,0:T(8,128)(2,1)} %get-tuple-element.20.refs_1_, ...), custom_call_target="tpu_custom_call" | custom-call | tf_op jit(solution)/shard_map/pallas_call | solution.py:675

commit v3 on v2

--- a/solution.py
+++ b/solution.py
@@ -1,3 +1,5 @@
+import functools
+
 import jax
 import jax.numpy as jnp
 from jax import lax
@@ -29,6 +31,8 @@
 LOG2E = 1.4426950408889634
 LN2 = 0.6931471805599453
 RESET = -1e4
+ACT_EARLY = ((2, 0), (2, 1))
+ACT_LATE = ((1, 0), (3, 0), (1, 1), (3, 1))
 
 
 def slots_of(chains):
@@ -65,15 +69,14 @@
     bd_ref,
     logit_ref,
     cot_hbm,
-    states_hbm,
-    grads_hbm,
+    states_v,
+    grads_v,
     wgi_ref,
     wgd_ref,
     vec_ref,
     act_v,
     cot_v,
     w_v,
-    actp,
     cotp,
     fac,
     psh,
@@ -81,22 +84,17 @@
     quo,
     gin,
     dgate,
+    direct,
     low_s,
-    st_s,
     u_s,
+    stage,
     reset_s,
     k8_s,
-    perm_s,
-    permt_s,
     seg_s,
-    states_v,
-    grads_v,
     part,
     prods,
-    pair_a,
-    pair_b,
-    gates_a,
-    gates_b,
+    in_a,
+    in_b,
     act_all,
     low_all,
     map_send,
@@ -112,7 +110,6 @@
     y2s,
     y2r,
     in_sem,
-    out_sem,
     small_sem,
     z1_ss,
     z1_rs,
@@ -124,6 +121,7 @@
     act_rs,
     low_ss,
     low_rs,
+    rep_rs,
 ):
     me = lax.axis_index("seq")
     y, z = me // RING_Z, lax.rem(me, RING_Z)
@@ -159,10 +157,6 @@
 
     lax.fori_loop(1, SEQ_DEVICES, hello, 0)
 
-    row = lax.broadcasted_iota(jnp.int32, (ROWS, ROWS), 0)
-    col = lax.broadcasted_iota(jnp.int32, (ROWS, ROWS), 1)
-    perm_s[...] = (col == (row & 7) * STEPS + (row >> 3)).astype(F32).astype(BF16)
-    permt_s[...] = (row == (col & 7) * STEPS + (col >> 3)).astype(F32).astype(BF16)
     seg = lax.broadcasted_iota(jnp.int32, (8, BW), 0)
     first = me * ROWS + seg * STEPS
     starts = [jnp.int32(0)]
@@ -179,40 +173,39 @@
     soft = jnp.maximum(logits, 0.0) + jnp.where(e < 0.0625, series, jnp.log(1.0 + e))
     k8_s[...] = -DECAY_SCALE * soft
 
-    def send_tile(src, dst, send_sem, recv_sem, to):
+    def send_tile(src, dst, send_sem, recv_sem, to, n=8):
         @pl.when(to != me)
         def _():
             pltpu.make_async_remote_copy(
-                src_ref=src.at[to],
-                dst_ref=dst.at[me],
+                src_ref=src.at[to, 0:n],
+                dst_ref=dst.at[me, 0:n],
                 send_sem=send_sem,
                 recv_sem=recv_sem,
                 device_id={"seq": to},
                 device_id_type=MESH,
             ).start()
 
-    def wait_tiles(buf, sem, n=8):
-        view = buf.at[pl.ds(0, SEQ_DEVICES - 1), 0:n]
+    def wait_tiles(buf, sem, n=8, count=SEQ_DEVICES - 1):
+        view = buf.at[pl.ds(0, count), 0:n]
         pltpu.make_async_copy(view, view, sem).wait()
 
     def lanes(h):
         return pl.ds(pl.multiple_of(h * BW, BW), BW)
 
-    def gate_dots(h, pair_s, gates_s):
+    def gate_dots(h, in_s):
         sl = lanes(h)
 
-        @pl.when(lax.rem(h, gh) == 0)
+        @pl.when((lax.rem(h, gh) == 0) & (h < HEADS - gh))
         def _():
             for c in fetch(h // gh):
                 c.wait()
 
-        pair = dot(perm_s[...], jnp.concatenate([act_v[:, sl], cot_v[:, sl]], axis=1))
-        pair_s[...] = pair
-        xb = pair[:, :BW].astype(BF16)
-        actp[h] = xb
-        gates_s[...] = dot(xb, w_v[h])
-
-    def local_maps(h, pair_s, gates_s):
+        xb = act_v[:, sl]
+        for t, v in enumerate((xb.astype(F32), cot_v[:, sl].astype(F32), dot(xb, w_v[h]))):
+            for i in range(v.shape[1] // ROWS):
+                in_s[2 * t + i] = v[:, i * ROWS : (i + 1) * ROWS]
+
+    def local_maps(h, in_s):
         sl = lanes(h)
         bi, bd = bi_ref[:, sl], bd_ref[:, sl]
         k8 = k8_s[:, sl] * LOG2E
@@ -221,11 +214,14 @@
         bwd = jnp.zeros((8, BW), F32)
         for k in range(STEPS):
             r = slice(8 * k, 8 * k + 8)
-            xk = pair_s[r, :BW]
-            ct = pair_s[r, BW:]
+            tokens = pl.ds(k, 8, stride=STEPS)
+            xk, ct, gi, gd = [
+                jnp.concatenate([in_s[t, tokens, :], in_s[t + 1, tokens, :]], axis=1)
+                for t in range(0, 8, 2)
+            ]
             cotp[h, r, :] = ct
-            ig = recip(1.0 + jnp.exp2((gates_s[r, :BW] + bi) * -LOG2E))
-            dg = recip(1.0 + jnp.exp2((gates_s[r, BW:] + bd) * -LOG2E))
+            ig = recip(1.0 + jnp.exp2((gi + bi) * -LOG2E))
+            dg = recip(1.0 + jnp.exp2((gd + bd) * -LOG2E))
             ld = dg * k8 + reset_s[r, :]
             f = jnp.exp2(ld)
             th = jnp.tanh(ld * -LN2)
@@ -266,30 +262,26 @@
             def _():
                 map_recv[me] = map_send[me]
 
-            send_tile(map_send, map_recv, small_sem.at[0], small_sem.at[1], to)
-        yd, q = h // (RING_Z // 2), lax.rem(h, RING_Z // 2)
-        d = lax.rem(yd - y + RING_Y, RING_Y)
-
-        @pl.when(d == 0)
-        def _():
-            act_all[q, 0] = actp[h]
-
-        @pl.when(d != 0)
-        def _():
-            pltpu.make_async_remote_copy(
-                src_ref=actp.at[h],
-                dst_ref=act_all.at[q, d],
-                send_sem=act_ss.at[q, d],
-                recv_sem=act_rs.at[q, d],
-                device_id={"seq": yd * RING_Z + z},
-                device_id_type=MESH,
-            ).start()
+            send_tile(map_send, map_recv, small_sem.at[0], small_sem.at[1], to, 3)
+
+    def act_copy(d, k):
+        yd = lax.rem(y + d, RING_Y)
+        wide = gw // 2
+        src = pl.ds(pl.multiple_of(yd * gw + k * wide, wide), wide)
+        return pltpu.make_async_remote_copy(
+            src_ref=act_v.at[:, src],
+            dst_ref=act_all.at[d, :, pl.ds(k * wide, wide)],
+            send_sem=act_ss.at[d, k],
+            recv_sem=act_rs.at[d, k],
+            device_id={"seq": yd * RING_Z + z},
+            device_id_type=MESH,
+        )
 
     def two_heads(i, carry):
-        gate_dots(2 * i + 1, pair_b, gates_b)
-        local_maps(2 * i, pair_a, gates_a)
-        gate_dots(2 * i + 2 - (2 * i + 2) // HEADS, pair_a, gates_a)
-        local_maps(2 * i + 1, pair_b, gates_b)
+        gate_dots(2 * i + 1, in_b)
+        local_maps(2 * i, in_a)
+        gate_dots(2 * i + 2 - (2 * i + 2) // HEADS, in_a)
+        local_maps(2 * i + 1, in_b)
         return carry
 
     def two_heads_and_share(i, carry):
@@ -299,12 +291,16 @@
             share(2 * i + k)
         return carry
 
-    gate_dots(0, pair_a, gates_a)
+    gate_dots(0, in_a)
     lax.fori_loop(0, HEADS // 4, two_heads, 0)
     pl.semaphore_wait(barrier, SEQ_DEVICES - 1)
+    for c in fetch(GROUPS - 1):
+        c.wait()
+    for d, k in ACT_EARLY:
+        act_copy(d, k).start()
     lax.fori_loop(HEADS // 4, HEADS // 2, two_heads_and_share, 0)
 
-    wait_tiles(map_recv, small_sem.at[1])
+    wait_tiles(map_recv, small_sem.at[1], 3)
     hid = jnp.zeros((1, ROWS), F32)
     for s in range(SEQ_DEVICES):
         rep_send[s, 0:1, :] = hid
@@ -315,20 +311,33 @@
         back = map_recv[s, 0:1, :] * back + map_recv[s, 2:3, :]
     rep_recv[me, 0:2] = rep_send[me, 0:2]
 
-    def reply(i, carry):
-        to = lax.rem(me + i, SEQ_DEVICES)
-        pltpu.make_async_remote_copy(
-            src_ref=rep_send.at[to, 0:2],
-            dst_ref=rep_recv.at[me, 0:2],
-            send_sem=small_sem.at[2],
-            recv_sem=small_sem.at[3],
-            device_id={"seq": to},
-            device_id_type=MESH,
-        ).start()
+    zp, odd = z // 2, lax.rem(z, 2)
+
+    def turns(j, parity):
+        return (2, 1 + 2 * parity, 3 - 2 * parity, 0)[j]
+
+    def reply(j, i, carry):
+        parity = lax.rem(i, 2)
+        tz = 2 * lax.rem(zp + RING_Z // 2 - turns(j, parity), RING_Z // 2) + parity
+        to = i // 2 * RING_Z + tz
+
+        @pl.when(to != me)
+        def _():
+            pltpu.make_async_remote_copy(
+                src_ref=rep_send.at[to, 0:2],
+                dst_ref=rep_recv.at[me, 0:2],
+                send_sem=small_sem.at[2],
+                recv_sem=rep_rs.at[j],
+                device_id={"seq": to},
+                device_id_type=MESH,
+            ).start()
+
         return carry
 
-    lax.fori_loop(1, SEQ_DEVICES, reply, 0)
-    wait_tiles(rep_recv, small_sem.at[3], 2)
+    for j in range(4):
+        lax.fori_loop(0, 2 * RING_Y, functools.partial(reply, j), 0)
+    for d, k in ACT_LATE:
+        act_copy(d, k).start()
 
     def chains(h):
         sl = lanes(h)
@@ -346,7 +355,6 @@
         sum_i = jnp.zeros((8, BW), F32)
         sum_d = jnp.zeros((8, BW), F32)
         sum_l = jnp.zeros((8, BW), F32)
-        hids, lows_i, lows_d = [], [], []
         for k in range(STEPS):
             r = slice(8 * k, 8 * k + 8)
             u = u_s[r, :]
@@ -359,16 +367,18 @@
             sum_i = sum_i + pi
             sum_d = sum_d + pd
             sum_l = sum_l + dl
-            hids.append(hid)
-            lows_i.append(pi)
-            lows_d.append(pd)
-            coef[h, r, :] = u * coef[h, r, :]
-        low_i = jnp.concatenate(lows_i, axis=0).astype(BF16)
-        low_d = jnp.concatenate(lows_d, axis=0).astype(BF16)
-        st_s[h] = jnp.concatenate(hids, axis=0).astype(BF16)
-        both = jnp.concatenate([low_i, low_d], axis=1)
+            tokens = pl.ds(k, 8, stride=STEPS)
+            du = u * coef[h, r, :]
+            for t in range(2):
+                cols = slice(t * ROWS, (t + 1) * ROWS)
+                stage[t, tokens, :] = pi[:, cols]
+                stage[2 + t, tokens, :] = pd[:, cols]
+                stage[4 + t, tokens, :] = hid[:, cols]
+                direct[2 * h + t, tokens, :] = du[:, cols]
+        both = jnp.concatenate([stage[t] for t in range(4)], axis=1).astype(BF16)
         low_s[h] = both
-        wg = dot(actp[h], both[:, YZ:], ((0,), (0,)))
+        states_v[:, sl] = jnp.concatenate([stage[4], stage[5]], axis=1).astype(BF16)
+        wg = dot(act_v[:, sl], both[:, YZ:], ((0,), (0,)))
         part[2 * h] = wg[:ROWS]
         part[2 * h + 1] = wg[ROWS:]
         sums = tile_of(
@@ -385,23 +395,18 @@
 
             send_tile(bias_send, bias_recv, small_sem.at[4], small_sem.at[5], to)
 
-    zp, odd = z // 2, lax.rem(z, 2)
-
     def group_of(j):
-        return lax.rem(zp + (2, 1 + 2 * odd, 3 - 2 * odd, 0)[j], RING_Z // 2)
+        return lax.rem(zp + turns(j, odd), RING_Z // 2)
 
     def make_group(j):
         q = group_of(j)
+        wait_tiles(rep_recv, rep_rs.at[j], 2, 2 * RING_Y - (j == 3))
 
         def one(i, carry):
             d = lax.rem(i + 2, RING_Y)
             yd = lax.rem(y + d, RING_Y)
             h = yd * (RING_Z // 2) + q
             chains(h)
-
-            @pl.when(d == 0)
-            def _():
-                low_all[q, 0] = low_s[h, :, :YZ]
 
             @pl.when(d != 0)
             def _():
@@ -420,10 +425,9 @@
 
     def finish(h, carry):
         sl = lanes(h)
-        ig = coef[h] + dot(low_s[h], w_v[h], ((1,), (1,)))
-        out = dot(permt_s[...], jnp.concatenate([st_s[h], ig.astype(BF16)], axis=1)).astype(BF16)
-        states_v[:, sl] = out[:, :BW]
-        grads_v[:, sl] = out[:, BW:]
+        mine = jnp.concatenate([direct[2 * h], direct[2 * h + 1]], axis=1)
+        ig = mine + dot(low_s[h], w_v[h], ((1,), (1,)))
+        grads_v[:, sl] = ig.astype(BF16)
         return carry
 
     def finish_quarter(i):
@@ -492,13 +496,15 @@
 
     def product(j):
         q = group_of(j)
+        if j == 0:
+            for d, k in ACT_EARLY + ACT_LATE:
+                act_copy(d, k).wait_recv()
         for d in range(1, RING_Y):
-            if j == 0:
-                for k in range(RING_Z // 2):
-                    landed(act_all.at[k, d], act_rs.at[k, d])
             landed(low_all.at[q, d], low_rs.at[j, d])
-        acts = act_all[q].reshape(RING_Y * ROWS, BW)
-        lows = low_all[q].reshape(RING_Y * ROWS, YZ)
+        h = y * (RING_Z // 2) + q
+        acts = [act_v[:, lanes(h)]] + [act_all[d, :, lanes(q)] for d in range(1, RING_Y)]
+        lows = [low_s[h, :, :YZ]] + [low_all[q, d] for d in range(1, RING_Y)]
+        acts, lows = jnp.concatenate(acts, axis=0), jnp.concatenate(lows, axis=0)
         wg = dot(acts, lows, ((0,), (0,)))
         prods[2 * q] = wg[:ROWS]
         prods[2 * q + 1] = wg[ROWS:]
@@ -542,12 +548,6 @@
     product(2)
     z2_step(2)
     finish_quarter(3)
-    stores = [
-        pltpu.make_async_copy(states_v, states_hbm, out_sem.at[0]),
-        pltpu.make_async_copy(grads_v, grads_hbm, out_sem.at[1]),
-    ]
-    for c in stores:
-        c.start()
     product(3)
     z2_step(1)
 
@@ -574,15 +574,14 @@
 
     for s in sends:
         s.wait_send()
+    for d, k in ACT_EARLY + ACT_LATE:
+        act_copy(d, k).wait_send()
     for d in range(1, RING_Y):
         for k in range(RING_Z // 2):
-            landed(act_all.at[k, d], act_ss.at[k, d])
             landed(low_all.at[k, d], low_ss.at[k, d])
-    wait_tiles(map_send, small_sem.at[0])
+    wait_tiles(map_send, small_sem.at[0], 3)
     wait_tiles(rep_send, small_sem.at[2], 2)
     wait_tiles(bias_send, small_sem.at[4])
-    for c in stores:
-        c.wait()
 
 
 def hand_over(*refs):
@@ -605,31 +604,19 @@
         pltpu.VMEM((ROWS, WIDTH), BF16),
         pltpu.VMEM((ROWS, WIDTH), BF16),
         pltpu.VMEM((HEADS, BW, 2 * BW), BF16),
-        pltpu.VMEM(chunk, BF16),
-        pltpu.VMEM(chunk, F32),
-        pltpu.VMEM(chunk, F32),
-        pltpu.VMEM(chunk, F32),
-        pltpu.VMEM(chunk, F32),
-        pltpu.VMEM(chunk, F32),
-        pltpu.VMEM(chunk, F32),
-        pltpu.VMEM(chunk, F32),
+        *[pltpu.VMEM(chunk, F32)] * 7,
+        pltpu.VMEM((2 * HEADS, ROWS, ROWS), F32),
         pltpu.VMEM((HEADS, ROWS, 2 * BW), BF16),
-        pltpu.VMEM(chunk, BF16),
         pltpu.VMEM((ROWS, BW), F32),
+        pltpu.VMEM((6, ROWS, ROWS), F32),
         pltpu.VMEM((ROWS, BW), F32),
         pltpu.VMEM((1, WIDTH), F32),
-        pltpu.VMEM((ROWS, ROWS), BF16),
-        pltpu.VMEM((ROWS, ROWS), BF16),
         pltpu.VMEM((HEADS, 4, 8, BW), F32),
-        pltpu.VMEM((ROWS, WIDTH), BF16),
-        pltpu.VMEM((ROWS, WIDTH), BF16),
         pltpu.VMEM((SEQ_DEVICES, ROWS, ZY), F32),
         pltpu.VMEM((RING_Z, ROWS, YZ), F32),
-        pltpu.VMEM((ROWS, 2 * BW), F32),
-        pltpu.VMEM((ROWS, 2 * BW), F32),
-        pltpu.VMEM((ROWS, 2 * BW), F32),
-        pltpu.VMEM((ROWS, 2 * BW), F32),
-        pltpu.VMEM((RING_Z // 2, RING_Y, ROWS, BW), BF16),
+        pltpu.VMEM((8, ROWS, ROWS), F32),
+        pltpu.VMEM((8, ROWS, ROWS), F32),
+        pltpu.VMEM((RING_Y, ROWS, WIDTH // RING_Y), BF16),
         pltpu.VMEM((RING_Z // 2, RING_Y, ROWS, YZ), BF16),
     ]
     scratch += [pltpu.VMEM((SEQ_DEVICES, 8, ROWS), F32) for _ in range(6)]
@@ -641,23 +628,23 @@
         scratch += [pltpu.VMEM(shape, BF16), pltpu.VMEM(shape, BF16)]
     scratch += [
         pltpu.SemaphoreType.DMA((GROUPS, 4)),
-        pltpu.SemaphoreType.DMA((2,)),
         pltpu.SemaphoreType.DMA((6,)),
     ]
     quads = (RING_Z // 2, RING_Y)
-    for shape in ((Z_COUNT,), (Z_COUNT,), (RING_Y,), quads, quads):
+    for shape in ((Z_COUNT,), (Z_COUNT,), (RING_Y,), (RING_Y, 2), quads):
         scratch += [pltpu.SemaphoreType.DMA(shape), pltpu.SemaphoreType.DMA(shape)]
-    states, grads, wgi, wgd, vec = pl.pallas_call(
+    scratch.append(pltpu.SemaphoreType.DMA((4,)))
+    results = pl.pallas_call(
         kernel,
         out_shape=(
-            jax.ShapeDtypeStruct((ROWS, WIDTH), BF16),
-            jax.ShapeDtypeStruct((ROWS, WIDTH), BF16),
-            jax.ShapeDtypeStruct((ROWS, BW), F32),
-            jax.ShapeDtypeStruct((ROWS, BW), F32),
-            jax.ShapeDtypeStruct((8, ROWS), F32),
+            pltpu.VMEM((ROWS, WIDTH), BF16),
+            pltpu.VMEM((ROWS, WIDTH), BF16),
+            pltpu.VMEM((ROWS, BW), F32),
+            pltpu.VMEM((ROWS, BW), F32),
+            pltpu.VMEM((8, ROWS), F32),
         ),
         in_specs=[smem, any_spec, any_spec, any_spec, vmem, vmem, vmem, any_spec],
-        out_specs=(any_spec, any_spec, vmem, vmem, vmem),
+        out_specs=(vmem,) * 5,
         scratch_shapes=scratch,
         compiler_params=pltpu.CompilerParams(
             collective_id=0, has_side_effects=True, vmem_limit_bytes=60 * 1024 * 1024
@@ -672,14 +659,15 @@
         logits.reshape(1, WIDTH),
         cot,
     )
+    results = [pltpu.with_memory_space_constraint(r, pltpu.VMEM) for r in results]
     outs = pl.pallas_call(
         hand_over,
-        out_shape=[jax.ShapeDtypeStruct(a.shape, a.dtype) for a in (states, grads, wgi, wgd)]
+        out_shape=[jax.ShapeDtypeStruct(a.shape, a.dtype) for a in results[:4]]
         + [jax.ShapeDtypeStruct((1, ROWS), F32)] * 3,
         in_specs=[vmem] * 5,
         out_specs=[any_spec] * 7,
         scratch_shapes=[pltpu.SemaphoreType.DMA((7,))],
-    )(states, grads, wgi, wgd, vec)
+    )(*results)
     return (*outs[:4], *(v.reshape(ROWS) for v in outs[4:]))
 
 

time: 65.5 us -> 57.9 us (0.88)
  Pallas kernels: 64.7 us -> 57.1 us
    pallas_call x1, Pallas kernels: 61.7 us -> 55.6 us  [on_device(): pl.pallas_call(kernel, out_shape=(pltpu.VMEM((ROWS, WIDTH), BF16), pltpu....]
    pallas_call x1, Pallas kernels: 3.04 us -> 1.46 us  [on_device(): pl.pallas_call(hand_over, out_shape=[jax.ShapeDtypeStruct(a.shape, a.dtyp...]
where the time goes in v3:
time: 57.9 us; the launch traced here: 57.7 us
  Pallas kernels  57.1 us (99%)
  between operations  0.64 us (1%)
    pallas_call x1, Pallas kernels, on_device(): pl.pallas_call(kernel, out_shape=(pltpu.VMEM((ROWS, WIDTH), BF16), pltpu....  55.6 us
    pallas_call x1, Pallas kernels, on_device(): pl.pallas_call(hand_over, out_shape=[jax.ShapeDtypeStruct(a.shape, a.dtyp...  1.46 us

profile of v3, /device:TPU:2, one launch (start us, length us, event | category | flops | bytes accessed | tf_op | source)
XLA Modules:
  0.0 57.7 jit_solution(2374705315712778972)
XLA Ops:
  0.6 55.6 %shard_map.135 = (bf16[128,4096]{1,0:T(8,128)(2,1)S(1)}, bf16[128,4096]{1,0:T(8,128)(2,1)S(1)}, f32[128,256]{1,0:T(8,128)S(1)}, f32[128,256]{1,0:T(8,128)S(1)}, f32[8,128]{1,0:T(8,128)S(1)}) custom-call(s32[6]{0:T(128)} %docs_ref.1, bf16[128,4096]{1,0:T(8,128)(2,1)} %act_hbm.1, bf16[16,256,256]{2,1,0:T(8,128)(2,1)} %wi_hbm.1, bf16[16,256,256]{2,1,0:T(8,128)(2,1)} %wd_hbm.1, ...), custom_call_target="tpu_custom_call" | custom-call | tf_op jit(solution)/shard_map/pallas_call | solution.py:637
  56.3 1.5 %shard_map.136 = (bf16[128,4096]{1,0:T(8,128)(2,1)}, bf16[128,4096]{1,0:T(8,128)(2,1)}, f32[128,256]{1,0:T(8,128)}, f32[128,256]{1,0:T(8,128)}, f32[1,128]{1,0:T...) custom-call(bf16[128,4096]{1,0:T(8,128)(2,1)S(1)} %get-tuple-element.19.refs_0_, ...), custom_call_target="tpu_custom_call" | custom-call | tf_op jit(solution)/shard_map/pallas_call | solution.py:663

commit v4 on v3

--- a/solution.py
+++ b/solution.py
@@ -19,7 +19,8 @@
 GROUPS = 4
 ZY = 128
 YZ = 2 * BW - ZY
-HALF = ROWS // 2
+PIECES = 2
+PIECE = ROWS // PIECES
 DECAY_SCALE = 8.0
 ROOT_LIMIT = 2000.0
 TINY = 1.2e-38
@@ -27,12 +28,11 @@
 F32 = jnp.float32
 BF16 = jnp.bfloat16
 
-Z_CHAINS = ((0, 1, 4), (0, -1, 3), (1, 1, 3), (1, -1, 4))
+Z_CHAINS = tuple((p, way, 3 + ((p % 2 == 0) == (way > 0))) for p in range(PIECES) for way in (1, -1))
 LOG2E = 1.4426950408889634
 LN2 = 0.6931471805599453
 RESET = -1e4
-ACT_EARLY = ((2, 0), (2, 1))
-ACT_LATE = ((1, 0), (3, 0), (1, 1), (3, 1))
+ACT_EARLY, ACT_NEXT, ACT_LATE = (0,), (1, 2), (3,)
 
 
 def slots_of(chains):
@@ -264,18 +264,29 @@
 
             send_tile(map_send, map_recv, small_sem.at[0], small_sem.at[1], to, 3)
 
-    def act_copy(d, k):
-        yd = lax.rem(y + d, RING_Y)
-        wide = gw // 2
-        src = pl.ds(pl.multiple_of(yd * gw + k * wide, wide), wide)
+    zp, odd = z // 2, lax.rem(z, 2)
+
+    def turns(j, parity):
+        return (2, 1 + 2 * parity, 3 - 2 * parity, 0)[j]
+
+    def group_of(j):
+        return lax.rem(zp + turns(j, odd), RING_Z // 2)
+
+    def act_copy(d, j):
+        yd, q = lax.rem(y + d, RING_Y), group_of(j)
         return pltpu.make_async_remote_copy(
-            src_ref=act_v.at[:, src],
-            dst_ref=act_all.at[d, :, pl.ds(k * wide, wide)],
-            send_sem=act_ss.at[d, k],
-            recv_sem=act_rs.at[d, k],
+            src_ref=act_v.at[:, lanes(yd * (RING_Z // 2) + q)],
+            dst_ref=act_all.at[d, :, lanes(q)],
+            send_sem=act_ss.at[d, j],
+            recv_sem=act_rs.at[d, j],
             device_id={"seq": yd * RING_Z + z},
             device_id_type=MESH,
         )
+
+    def act_send(groups):
+        for j in groups:
+            for d in (2, 3, 1):
+                act_copy(d, j).start()
 
     def two_heads(i, carry):
         gate_dots(2 * i + 1, in_b)
@@ -296,8 +307,7 @@
     pl.semaphore_wait(barrier, SEQ_DEVICES - 1)
     for c in fetch(GROUPS - 1):
         c.wait()
-    for d, k in ACT_EARLY:
-        act_copy(d, k).start()
+    act_send(ACT_EARLY)
     lax.fori_loop(HEADS // 4, HEADS // 2, two_heads_and_share, 0)
 
     wait_tiles(map_recv, small_sem.at[1], 3)
@@ -311,11 +321,6 @@
         back = map_recv[s, 0:1, :] * back + map_recv[s, 2:3, :]
     rep_recv[me, 0:2] = rep_send[me, 0:2]
 
-    zp, odd = z // 2, lax.rem(z, 2)
-
-    def turns(j, parity):
-        return (2, 1 + 2 * parity, 3 - 2 * parity, 0)[j]
-
     def reply(j, i, carry):
         parity = lax.rem(i, 2)
         tz = 2 * lax.rem(zp + RING_Z // 2 - turns(j, parity), RING_Z // 2) + parity
@@ -336,8 +341,7 @@
 
     for j in range(4):
         lax.fori_loop(0, 2 * RING_Y, functools.partial(reply, j), 0)
-    for d, k in ACT_LATE:
-        act_copy(d, k).start()
+    act_send(ACT_NEXT)
 
     def chains(h):
         sl = lanes(h)
@@ -395,33 +399,39 @@
 
             send_tile(bias_send, bias_recv, small_sem.at[4], small_sem.at[5], to)
 
-    def group_of(j):
-        return lax.rem(zp + turns(j, odd), RING_Z // 2)
-
-    def make_group(j):
+    def low_copy(j, d):
+        q = group_of(j)
+        yd = lax.rem(y + d, RING_Y)
+        return pltpu.make_async_remote_copy(
+            src_ref=low_s.at[yd * (RING_Z // 2) + q, :, pl.ds(0, YZ)],
+            dst_ref=low_all.at[q, d],
+            send_sem=low_ss.at[j, d],
+            recv_sem=low_rs.at[j, d],
+            device_id={"seq": yd * RING_Z + z},
+            device_id_type=MESH,
+        )
+
+    def make_group(j, send):
         q = group_of(j)
         wait_tiles(rep_recv, rep_rs.at[j], 2, 2 * RING_Y - (j == 3))
 
         def one(i, carry):
             d = lax.rem(i + 2, RING_Y)
-            yd = lax.rem(y + d, RING_Y)
-            h = yd * (RING_Z // 2) + q
-            chains(h)
-
-            @pl.when(d != 0)
-            def _():
-                pltpu.make_async_remote_copy(
-                    src_ref=low_s.at[h, :, pl.ds(0, YZ)],
-                    dst_ref=low_all.at[q, d],
-                    send_sem=low_ss.at[j, d],
-                    recv_sem=low_rs.at[j, d],
-                    device_id={"seq": yd * RING_Z + z},
-                    device_id_type=MESH,
-                ).start()
+            chains(lax.rem(y + d, RING_Y) * (RING_Z // 2) + q)
+
+            if send:
+
+                @pl.when(d != 0)
+                def _():
+                    low_copy(j, d).start()
 
             return carry
 
         lax.fori_loop(0, RING_Y, one, 0)
+
+    def send_group(j):
+        for d in (2, 3, 1):
+            low_copy(j, d).start()
 
     def finish(h, carry):
         sl = lanes(h)
@@ -433,11 +443,8 @@
     def finish_quarter(i):
         lax.fori_loop(i * HEADS // 4, (i + 1) * HEADS // 4, finish, 0)
 
-    def half(p):
-        return slice(p * HALF, (p + 1) * HALF)
-
-    def landed(buf, sem):
-        pltpu.make_async_copy(buf, buf, sem).wait()
+    def piece_of(p):
+        return slice(p * PIECE, (p + 1) * PIECE)
 
     def z_at(off):
         return lax.rem(z + off + RING_Z, RING_Z)
@@ -469,7 +476,7 @@
         if i:
             z1[(c, i - 1)].wait_recv()
         for d in range(RING_Y):
-            v = part[y_at(d) * RING_Z + zd, half(p), :]
+            v = part[y_at(d) * RING_Z + zd, piece_of(p), :]
             if i:
                 v = v + z1r[n - 1, d].astype(F32)
             z1s[n, d] = v.astype(BF16)
@@ -481,26 +488,24 @@
     def z1_fin():
         for c, (p, way, hops) in enumerate(Z_CHAINS):
             z1[(c, hops - 1)].wait_recv()
-        for p in range(2):
+        for p in range(PIECES):
             n, m = last_of(p)
             for d in range(RING_Y):
-                v = part[y_at(d) * RING_Z + z, half(p), :] + (
+                v = part[y_at(d) * RING_Z + z, piece_of(p), :] + (
                     z1r[n, d].astype(F32) + z1r[m, d].astype(F32)
                 )
                 if d:
-                    y2s[d, half(p), :] = v.astype(BF16)
+                    y2s[d, piece_of(p), :] = v.astype(BF16)
                 else:
-                    part[me, half(p), :] = v
+                    part[me, piece_of(p), :] = v
         for d in (2, 1, 3):
             y2[d] = launch(y2s.at[d], y2r.at[d], y2_ss.at[d], y2_rs.at[d], y_at(d), z)
 
     def product(j):
         q = group_of(j)
-        if j == 0:
-            for d, k in ACT_EARLY + ACT_LATE:
-                act_copy(d, k).wait_recv()
         for d in range(1, RING_Y):
-            landed(low_all.at[q, d], low_rs.at[j, d])
+            act_copy(d, j).wait_recv()
+            low_copy(j, d).wait_recv()
         h = y * (RING_Z // 2) + q
         acts = [act_v[:, lanes(h)]] + [act_all[d, :, lanes(q)] for d in range(1, RING_Y)]
         lows = [low_s[h, :, :YZ]] + [low_all[q, d] for d in range(1, RING_Y)]
@@ -517,36 +522,39 @@
             n = Z_SLOT[(c, i)]
             if i:
                 z2[(c, i - 1)].wait_recv()
-            v = prods[z_at(way * distance), half(p), :]
+            v = prods[z_at(way * distance), piece_of(p), :]
             if i:
                 v = v + z2r[n - 1].astype(F32)
             z2s[n] = v.astype(BF16)
             z2[(c, i)] = launch(z2s.at[n], z2r.at[n], z2_ss.at[n], z2_rs.at[n], y, z_at(way))
 
-    def z1_sends(*which):
-        for c, i in which:
-            z1_send(c, i)
-
-    make_group(0)
-    z1_sends((0, 0), (3, 0))
-    make_group(1)
-    z1_sends((1, 0), (2, 0))
-    make_group(2)
-    z1_sends((0, 1), (3, 1))
-    make_group(3)
-    z1_sends((1, 1), (2, 1))
+    def z1_step(distance, hops=(4, 3)):
+        for c, chain in enumerate(Z_CHAINS):
+            if chain[2] in hops and chain[2] >= distance:
+                z1_send(c, chain[2] - distance)
+
+    make_group(0, True)
+    z1_step(4)
+    make_group(1, True)
+    z1_step(3, (3,))
+    make_group(2, False)
+    z1_step(3, (4,))
     product(0)
     z2_step(4)
-    z1_sends((0, 2), (3, 2))
-    finish_quarter(0)
-    z1_sends((1, 2), (2, 2), (0, 3), (3, 3))
+    send_group(2)
+    make_group(3, False)
+    z1_step(2)
     product(1)
     z2_step(3)
+    act_send(ACT_LATE)
+    send_group(3)
+    finish_quarter(0)
+    z1_step(1)
     finish_quarter(1)
-    z1_fin()
-    finish_quarter(2)
     product(2)
     z2_step(2)
+    finish_quarter(2)
+    z1_fin()
     finish_quarter(3)
     product(3)
     z2_step(1)
@@ -566,19 +574,19 @@
     wgd_ref[:, 2 * BW - YZ :] = rest
     for c, (p, way, hops) in enumerate(Z_CHAINS):
         z2[(c, hops - 1)].wait_recv()
-    for p in range(2):
+    for p in range(PIECES):
         n, m = last_of(p)
-        done = prods[z, half(p), :] + (z2r[n].astype(F32) + z2r[m].astype(F32))
-        wgi_ref[half(p), :] = done[:, :BW]
-        wgd_ref[half(p), : YZ - BW] = done[:, BW:]
+        done = prods[z, piece_of(p), :] + (z2r[n].astype(F32) + z2r[m].astype(F32))
+        wgi_ref[piece_of(p), :] = done[:, :BW]
+        wgd_ref[piece_of(p), : YZ - BW] = done[:, BW:]
 
     for s in sends:
         s.wait_send()
-    for d, k in ACT_EARLY + ACT_LATE:
-        act_copy(d, k).wait_send()
     for d in range(1, RING_Y):
-        for k in range(RING_Z // 2):
-            landed(low_all.at[k, d], low_ss.at[k, d])
+        for j in range(RING_Z // 2):
+            act_copy(d, j).wait_send()
+        for j in range(RING_Z // 2):
+            low_copy(j, d).wait_send()
     wait_tiles(map_send, small_sem.at[0], 3)
     wait_tiles(rep_send, small_sem.at[2], 2)
     wait_tiles(bias_send, small_sem.at[4])
@@ -621,8 +629,8 @@
     ]
     scratch += [pltpu.VMEM((SEQ_DEVICES, 8, ROWS), F32) for _ in range(6)]
     for shape in (
-        (Z_COUNT, RING_Y, HALF, ZY),
-        (Z_COUNT, HALF, YZ),
+        (Z_COUNT, RING_Y, PIECE, ZY),
+        (Z_COUNT, PIECE, YZ),
         (RING_Y, ROWS, ZY),
     ):
         scratch += [pltpu.VMEM(shape, BF16), pltpu.VMEM(shape, BF16)]
@@ -631,7 +639,7 @@
         pltpu.SemaphoreType.DMA((6,)),
     ]
     quads = (RING_Z // 2, RING_Y)
-    for shape in ((Z_COUNT,), (Z_COUNT,), (RING_Y,), (RING_Y, 2), quads):
+    for shape in ((Z_COUNT,), (Z_COUNT,), (RING_Y,), quads, quads):
         scratch += [pltpu.SemaphoreType.DMA(shape), pltpu.SemaphoreType.DMA(shape)]
     scratch.append(pltpu.SemaphoreType.DMA((4,)))
     results = pl.pallas_call(

time: 57.9 us -> 57.3 us (0.990)
  Pallas kernels: 57.1 us -> 56.5 us
where the time goes in v4:
time: 57.3 us; the launch traced here: 57.1 us
  Pallas kernels  56.5 us (99%)
  between operations  0.64 us (1%)
    pallas_call x1, Pallas kernels, on_device(): pl.pallas_call(kernel, out_shape=(pltpu.VMEM((ROWS, WIDTH), BF16), pltpu....  55 us
    pallas_call x1, Pallas kernels, on_device(): pl.pallas_call(hand_over, out_shape=[jax.ShapeDtypeStruct(a.shape, a.dtyp...  1.46 us

profile of v4, /device:TPU:2, one launch (start us, length us, event | category | flops | bytes accessed | tf_op | source)
XLA Modules:
  0.0 57.1 jit_solution(10905791043380312432)
XLA Ops:
  0.6 55.0 %shard_map.135 = (bf16[128,4096]{1,0:T(8,128)(2,1)S(1)}, bf16[128,4096]{1,0:T(8,128)(2,1)S(1)}, f32[128,256]{1,0:T(8,128)S(1)}, f32[128,256]{1,0:T(8,128)S(1)}, f32[8,128]{1,0:T(8,128)S(1)}) custom-call(s32[6]{0:T(128)} %docs_ref.1, bf16[128,4096]{1,0:T(8,128)(2,1)} %act_hbm.1, bf16[16,256,256]{2,1,0:T(8,128)(2,1)} %wi_hbm.1, bf16[16,256,256]{2,1,0:T(8,128)(2,1)} %wd_hbm.1, ...), custom_call_target="tpu_custom_call" | custom-call | tf_op jit(solution)/shard_map/pallas_call | solution.py:645
  55.7 1.5 %shard_map.136 = (bf16[128,4096]{1,0:T(8,128)(2,1)}, bf16[128,4096]{1,0:T(8,128)(2,1)}, f32[128,256]{1,0:T(8,128)}, f32[128,256]{1,0:T(8,128)}, f32[1,128]{1,0:T...) custom-call(bf16[128,4096]{1,0:T(8,128)(2,1)S(1)} %get-tuple-element.19.refs_0_, ...), custom_call_target="tpu_custom_call" | custom-call | tf_op jit(solution)/shard_map/pallas_call | solution.py:671
